TPU v7x, 512 devices: a whole 4x8x8 slice. The times are simulated.
512 devices in a mesh: seq: 32 (over z_hi, y), vocab: 16 (over x, z_lo, core).
Axes of the slice: x: 4, y: 8, z: 8 (z_hi: 4, z_lo: 2; z = z_hi * 2 + z_lo), core: 2. Of those that a mesh axis runs over, the one named last changes fastest.
Arguments:
- hidden: bfloat16 [2048, 5120], P('seq'), may hold values from -6 to 6
- norm_gain: float32 [5120], replicated, may hold values from 0.25 to 1.75
- head_weight: bfloat16 [4096, 5120], P('vocab'), may hold values from -1 to 1
- targets: int32 [2048], P('seq'), may hold values from 0 to 4095
- out_proj: bfloat16 [12288, 5120], P('seq', 'vocab'), may hold values from -0.078125 to 0.078125
- query: bfloat16 [2048, 12288], P(('seq', 'vocab')), may hold values from -6 to 6
- saved_key_value: bfloat16 [2, 2048, 1024], P(None, ('seq', 'vocab')), may hold values from -6 to 6
- offset: int32 [1], replicated, may hold values from 1 to 2047
Outputs:
- token_loss: float32 [2048], P('seq')
- hidden_grad: bfloat16 [2048, 5120], P('seq', 'vocab')
- query_grad: bfloat16 [2048, 12288], P(('seq', 'vocab'))
- key_value_gradient: bfloat16 [2, 2048, 1024], P(None, ('seq', 'vocab'))
All inputs are finite; a program needn't handle non-finite values.
Results may differ from a plain program's by a relative error of at most 0.039.
Values may be sent and summed in bfloat16 or wider, within the bound.
A program may use at most 64 MiB of HBM per device.

v0:
```python
import jax
import jax.numpy as jnp
from jax import lax
from jax.sharding import PartitionSpec as P

D = 5120
QUERY_HEAD_COUNT = 96
KEY_VALUE_HEADS = 8
HEAD_SIZE = 128


epsilon = 1e-05
loss_scaling = 32.0
masked_score = -1e30


def head_backward(q_rows, key_rows, value_rows, out_grad, q_position, k_position, doc_start):
    score_scale = q_rows.shape[-1] ** (-0.5)
    scores = (
        lax.dot_general(
            q_rows, key_rows, (((1,), (1,)), ((), ())), preferred_element_type=jnp.float32
        )
        * score_scale
    )
    visible = (k_position[None, :] <= q_position[:, None]) & (
        (k_position[None, :] >= doc_start) | (q_position[:, None] < doc_start)
    )
    scores = jnp.where(visible, scores, masked_score)
    peak_score = jnp.max(scores, axis=-1, keepdims=True)
    raised = jnp.exp(scores - peak_score)
    probs = raised / jnp.sum(raised, axis=-1, keepdims=True)
    probs_low = probs.astype(jnp.bfloat16)
    attended = jnp.dot(probs_low, value_rows, preferred_element_type=jnp.float32)
    row_delta = jnp.sum(out_grad.astype(jnp.float32) * attended, axis=-1, keepdims=True)
    prob_grad = lax.dot_general(
        out_grad, value_rows, (((1,), (1,)), ((), ())), preferred_element_type=jnp.float32
    )
    score_grad = (probs * (prob_grad - row_delta)).astype(jnp.bfloat16)
    query_part = (
        jnp.dot(score_grad, key_rows, preferred_element_type=jnp.float32) * score_scale
    ).astype(jnp.bfloat16)
    key_part = (
        lax.dot_general(
            score_grad, q_rows, (((0,), (0,)), ((), ())), preferred_element_type=jnp.float32
        )
        * score_scale
    )
    value_part = lax.dot_general(
        probs_low, out_grad, (((0,), (0,)), ((), ())), preferred_element_type=jnp.float32
    )
    return (query_part, key_part, value_part)


def shards(hidden, norm_gain, head_weight, targets, out_proj, query, saved_key_value, offset):
    sequence_count = lax.axis_size("seq")
    vocab_count = lax.axis_size("vocab")
    vocab_index = lax.axis_index("vocab")
    tok_rows = hidden.shape[0]
    inner_row_count = query.shape[0]
    local_heads = out_proj.shape[0] // HEAD_SIZE
    width = out_proj.shape[1]
    total_rows = tok_rows * sequence_count
    wide_hidden = hidden.astype(jnp.float32)
    inv_rms = lax.rsqrt(jnp.mean(wide_hidden * wide_hidden, axis=-1, keepdims=True) + epsilon)
    normed = (wide_hidden * inv_rms * norm_gain).astype(jnp.bfloat16)
    logits = lax.dot_general(
        normed, head_weight, (((1,), (1,)), ((), ())), preferred_element_type=jnp.float32
    )
    columns = vocab_index * head_weight.shape[0] + jnp.arange(head_weight.shape[0], dtype=jnp.int32)
    target_hit = targets[:, None] == columns[None, :]
    target_part = jnp.sum(jnp.where(target_hit, logits, jnp.float32(0.0)), axis=-1)
    row_peak = lax.pmax(jnp.max(logits, axis=-1), "vocab")
    local_total = jnp.sum(jnp.exp(logits - row_peak[:, None]), axis=-1)
    row_total, target_logit = lax.psum((local_total, target_part), "vocab")
    token_loss = jnp.log(row_total) + row_peak - target_logit
    probs = jnp.exp(logits - row_peak[:, None]) / row_total[:, None]
    logit_grad = (loss_scaling * (probs - target_hit.astype(jnp.float32))).astype(jnp.bfloat16)
    partial_grad = jnp.dot(logit_grad, head_weight, preferred_element_type=jnp.float32)
    normed_grad = lax.psum(partial_grad.astype(jnp.bfloat16), "vocab").astype(jnp.float32)
    gain_grad = normed_grad * norm_gain
    inner = jnp.sum(wide_hidden * gain_grad, axis=-1, keepdims=True)
    hidden_full = (inv_rms * gain_grad - wide_hidden * inv_rms**3 * inner / D).astype(jnp.bfloat16)
    hidden_slice = lax.dynamic_slice_in_dim(hidden_full, vocab_index * width, width, 1)
    projected = lax.dot_general(
        lax.all_gather(hidden_slice, "seq", axis=0, tiled=True),
        out_proj,
        (((1,), (1,)), ((), ())),
        preferred_element_type=jnp.float32,
    )
    grouped = projected.reshape(
        sequence_count, vocab_count, inner_row_count, local_heads * HEAD_SIZE
    )
    summed = lax.psum_scatter(
        grouped.astype(jnp.bfloat16), "vocab", scatter_dimension=1, tiled=True
    ).astype(jnp.float32)
    out_grad = summed.reshape(sequence_count * inner_row_count, local_heads, HEAD_SIZE).astype(
        jnp.bfloat16
    )
    moved = lax.all_to_all(
        query.reshape(inner_row_count, sequence_count, local_heads * HEAD_SIZE),
        "seq",
        split_axis=1,
        concat_axis=0,
        tiled=True,
    )
    moved = moved.reshape(sequence_count * inner_row_count, local_heads, HEAD_SIZE)
    pair_list = saved_key_value.reshape(2, inner_row_count, KEY_VALUE_HEADS, HEAD_SIZE)
    repetition_count = sequence_count // KEY_VALUE_HEADS
    spread = jnp.repeat(pair_list, repetition_count, axis=2)
    arrived = lax.all_to_all(spread, "seq", split_axis=2, concat_axis=1, tiled=True)
    blocks = lax.all_gather(
        arrived.reshape(2, sequence_count, 1, inner_row_count, HEAD_SIZE),
        "vocab",
        axis=2,
        tiled=True,
    )
    full_pairs = blocks.reshape(2, total_rows, HEAD_SIZE)
    q_position = (
        jnp.arange(sequence_count, dtype=jnp.int32)[:, None] * tok_rows
        + vocab_index * inner_row_count
        + jnp.arange(inner_row_count, dtype=jnp.int32)[None, :]
    ).reshape(-1)
    k_position = jnp.arange(total_rows, dtype=jnp.int32)
    doc_start = offset[0]

    def one_head(carry, inputs):
        q_rows, head_grad = inputs
        query_part, key_part, value_part = head_backward(
            q_rows, full_pairs[0], full_pairs[1], head_grad, q_position, k_position, doc_start
        )
        return ((carry[0] + key_part, carry[1] + value_part), query_part)

    zeros = jnp.zeros((total_rows, HEAD_SIZE), jnp.float32)
    accums, query_parts = lax.scan(
        one_head, (zeros, zeros), (moved.transpose(1, 0, 2), out_grad.transpose(1, 0, 2))
    )
    outgoing = query_parts.transpose(1, 0, 2).reshape(
        sequence_count, inner_row_count, local_heads * HEAD_SIZE
    )
    returned = lax.all_to_all(outgoing, "seq", split_axis=0, concat_axis=2, tiled=True)
    query_grad = returned.reshape(inner_row_count, QUERY_HEAD_COUNT * HEAD_SIZE)
    partial_pairs = jnp.stack([accums[0], accums[1]]).reshape(
        2, sequence_count, vocab_count, inner_row_count, HEAD_SIZE
    )
    pieces = lax.all_to_all(
        partial_pairs.astype(jnp.bfloat16), "vocab", split_axis=2, concat_axis=2, tiled=True
    ).astype(partial_pairs.dtype)
    folded = pieces.sum(axis=2)
    per_group_rows = lax.all_to_all(
        folded.astype(jnp.bfloat16), "seq", split_axis=1, concat_axis=1, tiled=True
    ).astype(folded.dtype)
    closing_sum = per_group_rows.reshape(
        2, KEY_VALUE_HEADS, repetition_count, inner_row_count, HEAD_SIZE
    ).sum(axis=2)
    key_value_gradient = (
        closing_sum.transpose(0, 2, 1, 3)
        .reshape(2, inner_row_count, KEY_VALUE_HEADS * HEAD_SIZE)
        .astype(jnp.bfloat16)
    )
    return (token_loss, hidden_slice, query_grad, key_value_gradient)


def solution(mesh):
    in_specs = (
        P("seq", None),
        P(),
        P("vocab", None),
        P("seq"),
        P("seq", "vocab"),
        P(("seq", "vocab"), None),
        P(None, ("seq", "vocab"), None),
        P(),
    )
    out_specs = (
        P("seq"),
        P("seq", "vocab"),
        P(("seq", "vocab"), None),
        P(None, ("seq", "vocab"), None),
    )
    return jax.shard_map(shards, mesh=mesh, in_specs=in_specs, out_specs=out_specs, check_vma=False)
```

profile of v0, /device:TPU:1, one launch (start us, length us, event | category | flops | bytes accessed | tf_op | source)
XLA Modules:
  0.0 505.1 jit_solution(7399547499309817417)
XLA Ops:
  11.4 33.4 %pmax.7 = f32[64]{0:T(128)S(1)} all-reduce(f32[64]{0:T(128)S(1)} %get-tuple-element.196), channel_id=1, replica_groups=mesh['seq'=32,'vocab'=16] {'vocab'}, use_global_device_ids=true, to_apply=%region_2.3 | all-reduce | flops 64 | bytes 512 | tf_op jit(solution)/shard_map/pmax | solution.py:72
  45.0 27.6 %all-reduce = (f32[64]{0:T(128)}, f32[64]{0:T(128)S(1)}) all-reduce(f32[64]{0:T(128)S(1)} %get-tuple-element.169, f32[64]{0:T(128)S(1)} %get-tuple-element.168), channel_id=1, replica_groups=mesh['seq'=32,'vocab'=16] {'vocab'}, use_global_device_ids=true, to_apply=%region_6.7 | all-reduce | flops 128 | bytes 1024 | tf_op jit(solution)/shard_map/psum | solution.py:74
  75.3 127.2 %all-reduce.3.cloned.1.call-done = bf16[64,5120]{1,0:T(8,128)(2,1)} async-done(((bf16[64,5120]{1,0:T(8,128)(2,1)}), bf16[64,5120]{1,0:T(8,128)(2,1)}) %all-reduce.3.cloned.1.call-update) | async-done | bytes 655376 | tf_op jit(solution)/shard_map/psum | solution.py:79
  206.5 22.6 %all_to_all.55 = bf16[2,4,32,128]{3,1,0,2:T(4,128)(2,1)S(1)} all-to-all(bf16[2,4,32,128]{3,1,0,2:T(4,128)(2,1)S(1)} %bitcast.103), channel_id=1, replica_groups=mesh['seq'=32,'vocab'=16] {'seq'}, dimensions={2} | all-to-all | bytes 131072 | tf_op jit(solution)/shard_map/all_to_all | solution.py:110
  229.8 59.8 %all-gather.4.cloned.1.call-done = bf16[2048,320]{1,0:T(8,128)(2,1)} async-done(((bf16[64,320]{1,0:T(8,128)(2,1)}), bf16[2048,320]{1,0:T(8,128)(2,1)}) %all-gather.4.cloned.1.call-update) | async-done | bytes 1310736 | tf_op jit(solution)/shard_map/all_gather | solution.py:85
  289.5 3.6 convolution_convert_fusion.1
  293.2 3.9 convert_element_type.65
  297.1 3.5 copy.53
  300.6 5.9 %all-to-all-start = ((bf16[4,32,384]{2,0,1:T(4,128)(2,1)}), bf16[4,32,384]{2,0,1:T(4,128)(2,1)S(1)}, u32[]{:S(2)}, u32[]{:S(2)}) async-start(bf16[4,32,384]{2,0,1:T(4,128)(2,1)} %bitcast.1), calls=%async_computation | async-start | bytes 196608 | tf_op jit(solution)/shard_map/all_to_all | solution.py:99
  306.5 11.4 %all-to-all-done = bf16[4,32,384]{2,0,1:T(4,128)(2,1)S(1)} async-done(((bf16[4,32,384]{2,0,1:T(4,128)(2,1)}), bf16[4,32,384]{2,0,1:T(4,128)(2,1)S(1)}, u32[]{:S(2)}, u32[]{:S(2)}) %all-to-all-start) | async-done | bytes 98336 | tf_op jit(solution)/shard_map/all_to_all | solution.py:99
  318.0 11.9 %all-gather.6.cloned.1.call-done = bf16[2,32,64,1,128]{4,1,3,0,2:T(8,128)(2,1)} async-done(((bf16[2,32,4,1,128]{4,1,3,0,2:T(8,128)(2,1)}), bf16[2,32,64,1,128]{4,1,3,0,2:T(8,128)(2,1)}) %all-gather.6.cloned.1.call-update) | async-done | bytes 1048592 | tf_op jit(solution)/shard_map/all_gather | solution.py:111
  329.9 2.9 copy.52
  332.8 65.8 %reduce-scatter.2.cloned.1.call-done = bf16[32,1,4,384]{3,0,2,1:T(8,128)(2,1)} async-done(((bf16[32,16,4,384]{3,0,2,1:T(8,128)(2,1)}), bf16[32,1,4,384]{3,0,2,1:T(8,128)(2,1)}) %reduce-scatter.2.cloned.1.call-update) | async-done | bytes 98320 | tf_op jit(solution)/shard_map/reduce_scatter | solution.py:93
  399.7 32.1 %while.16 = (s32[]{:T(128)}, f32[2048,128]{1,0:T(8,128)}, f32[2048,128]{1,0:T(8,128)}, bf16[3,128,128]{2,1,0:T(8,128)(2,1)S(1)}, s32[]{:T(128)}, /*index=5*/bf16...) while((s32[]{:T(128)}, f32[2048,128]{1,0:T(8,128)}, ...), condition=%wide.region_14.15_spmd.clone.clone, body=%wide.region_10.14_spmd.clone.clone.sunk | while | flops 409028480 | bytes 25900516 | solution.py:134
  404.1 2.8 convolution_add_fusion.2
  413.8 3.1 convolution_add_fusion.2
  417.8 2.6 fusion.98
  425.0 3.1 convolution_add_fusion.2
  435.8 7.3 %all-to-all-start.3 = ((bf16[2,32,16,4,128]{4,3,1,0,2:T(4,128)(2,1)}), bf16[2,32,16,4,128]{4,3,1,0,2:T(4,128)(2,1)}, u32[]{:S(2)}, u32[]{:S(2)}) async-start(bf16[2,32,16,4,128]{4,3,1,0,2:T(4,128)(2,1)} %copy.58), calls=%async_computation.4 | async-start | bytes 2097152 | tf_op jit(solution)/shard_map/all_to_all | solution.py:145
  443.9 15.2 %all-to-all-done.3 = bf16[2,32,16,4,128]{4,3,1,0,2:T(4,128)(2,1)} async-done(((bf16[2,32,16,4,128]{4,3,1,0,2:T(4,128)(2,1)}), bf16[2,32,16,4,128]{4,3,1,0,2:T(4,128)(2,1)}, u32[]{:S(2)}, u32[]{:S(2)}) %all-to-all-start.3) | async-done | bytes 1048608 | tf_op jit(solution)/shard_map/all_to_all | solution.py:145
  459.1 11.5 %all-to-all-start.2 = ((bf16[32,4,384]{2,1,0:T(4,128)(2,1)}), bf16[32,4,384]{2,1,0:T(4,128)(2,1)S(1)}, u32[]{:S(2)}, u32[]{:S(2)}) async-start(bf16[32,4,384]{2,1,0:T(4,128)(2,1)} %reshape.106), calls=%async_computation.3 | async-start | bytes 196608 | tf_op jit(solution)/shard_map/all_to_all | solution.py:140
  473.0 9.1 %all-to-all-done.2 = bf16[32,4,384]{2,1,0:T(4,128)(2,1)S(1)} async-done(((bf16[32,4,384]{2,1,0:T(4,128)(2,1)}), bf16[32,4,384]{2,1,0:T(4,128)(2,1)S(1)}, u32[]{:S(2)}, u32[]{:S(2)}) %all-to-all-start.2) | async-done | bytes 98336 | tf_op jit(solution)/shard_map/all_to_all | solution.py:140
  482.1 3.9 all-to-all-start.4
  486.5 10.8 %all-to-all-done.4 = bf16[2,32,4,128]{3,2,0,1:T(4,128)(2,1)S(1)} async-done(((bf16[2,32,4,128]{3,2,0,1:T(4,128)(2,1)}), bf16[2,32,4,128]{3,2,0,1:T(4,128)(2,1)S(1)}, u32[]{:S(2)}, u32[]{:S(2)}) %all-to-all-start.4) | async-done | bytes 65568 | tf_op jit(solution)/shard_map/all_to_all | solution.py:149
  (104 shorter events, 42.2 us)
Async XLA Ops:
  7.2 2.1 copy-start
  7.2 195.4 %all-reduce.3.cloned.1.call-start = ((), (), s32[]{:S(2)}) async-start(), calls=%async_computation.6 | async-start | bytes 1310720 | tf_op jit(solution)/shard_map/psum | solution.py:79
  9.2 35.5 %copy-start.8 = (s32[64]{0:T(128)S(1)}, s32[64]{0:T(128)}, u32[]{:S(2)}) copy-start(s32[64]{0:T(128)} %param.13) | copy-start | bytes 772
  72.6 1.6 copy-start.3
  74.1 128.5 %copy-start.7 = (f32[5120]{0:T(1024)S(1)}, f32[5120]{0:T(1024)}, u32[]{:S(2)}) copy-start(f32[5120]{0:T(1024)} %param.11) | copy-start | bytes 61444
  74.1 215.4 %all-gather.4.cloned.1.call-start = ((), (), s32[]{:S(2)}) async-start(), calls=%async_computation.7 | async-start | bytes 1622016 | tf_op jit(solution)/shard_map/all_gather | solution.py:85
  75.3 214.2 %copy-start.6 = (bf16[384,320]{0,1:T(8,128)(2,1)S(1)}, bf16[384,320]{0,1:T(8,128)(2,1)}, u32[]{:S(2)}) copy-start(bf16[384,320]{0,1:T(8,128)(2,1)} %param.14) | copy-start | bytes 737284
  202.5 1.4 copy-start.9
  205.7 124.2 %all-gather.6.cloned.1.call-start = ((), (), s32[]{:S(2)}) async-start(), calls=%async_computation.9 | async-start | bytes 1114112 | tf_op jit(solution)/shard_map/all_gather | solution.py:111
  229.7 168.9 %reduce-scatter.2.cloned.1.call-start = ((), (), s32[]{:S(2)}) async-start(), calls=%async_computation.8 | async-start | bytes 1671168 | tf_op jit(solution)/shard_map/reduce_scatter | solution.py:93
  300.6 17.3 %all-to-all-start = ((bf16[4,32,384]{2,0,1:T(4,128)(2,1)}), bf16[4,32,384]{2,0,1:T(4,128)(2,1)S(1)}, u32[]{:S(2)}, u32[]{:S(2)}) async-start(bf16[4,32,384]{2,0,1:T(4,128)(2,1)} %bitcast.1), calls=%async_computation | async-start | bytes 196608 | tf_op jit(solution)/shard_map/all_to_all | solution.py:99
  402.8 1.0 copy-start.1
  404.1 2.8 copy-start.2
  404.1 2.8 copy-start.5
  413.8 3.1 copy-start.2
  413.8 3.1 copy-start.5
  423.7 1.0 copy-start.1
  425.0 3.1 copy-start.2
  425.0 3.1 copy-start.5
  431.9 1.5 copy-start.4
  435.8 23.3 %all-to-all-start.3 = ((bf16[2,32,16,4,128]{4,3,1,0,2:T(4,128)(2,1)}), bf16[2,32,16,4,128]{4,3,1,0,2:T(4,128)(2,1)}, u32[]{:S(2)}, u32[]{:S(2)}) async-start(bf16[2,32,16,4,128]{4,3,1,0,2:T(4,128)(2,1)} %copy.58), calls=%async_computation.4 | async-start | bytes 2097152 | tf_op jit(solution)/shard_map/all_to_all | solution.py:145
  443.1 42.9 %copy-start.10 = (f32[64]{0:T(128)S(1)}, f32[64]{0:T(128)}, u32[]{:S(2)}) copy-start(f32[64]{0:T(128)} %get-tuple-element.188) | copy-start | bytes 772
  459.1 23.0 %all-to-all-start.2 = ((bf16[32,4,384]{2,1,0:T(4,128)(2,1)}), bf16[32,4,384]{2,1,0:T(4,128)(2,1)S(1)}, u32[]{:S(2)}, u32[]{:S(2)}) async-start(bf16[32,4,384]{2,1,0:T(4,128)(2,1)} %reshape.106), calls=%async_computation.3 | async-start | bytes 196608 | tf_op jit(solution)/shard_map/all_to_all | solution.py:140
  482.1 15.2 %all-to-all-start.4 = ((bf16[2,32,4,128]{3,2,0,1:T(4,128)(2,1)}), bf16[2,32,4,128]{3,2,0,1:T(4,128)(2,1)S(1)}, u32[]{:S(2)}, u32[]{:S(2)}) async-start(bf16[2,32,4,128]{3,2,0,1:T(4,128)(2,1)} %copy.59), calls=%async_computation.5 | async-start | bytes 131072 | tf_op jit(solution)/shard_map/all_to_all | solution.py:149
  (1 other events, 1.0 us)
Sparse Core Ops, SparseCore 0:
  74.2 128.2 all-reduce.2
  206.8 82.7 all-gather.3
  292.5 37.3 all-gather.5
  332.8 65.7 reduce-scatter.1
where the time goes:
time: 507 us; the launch traced here: 505 us
  waiting for transfers between devices  311 us (61%)
  blocking collectives  83.6 us (16%)
  matrix products  30.8 us (6%)
  starting transfers between devices  28.7 us (6%)
  local copies, waits for them, and re-layouts  20.6 us (4%)
  other arithmetic  15.9 us (3%)
  between operations  14 us (3%)
    psum x1, waiting for transfers between devices, shards(): lax.psum(partial_grad.astype(jnp.bfloat16), 'vocab').astype(jnp.float32)  127 us
    reduce_scatter x1, waiting for transfers between devices, shards(): lax.psum_scatter(grouped.astype(jnp.bfloat16), 'vocab', scatter_dimension...  65.8 us
    all_gather x1, waiting for transfers between devices, shards(): lax.all_gather(hidden_slice, 'seq', axis=0, tiled=True)  59.8 us
    pmax x1, blocking collectives, shards(): row_peak = lax.pmax(jnp.max(logits, axis=-1), 'vocab')  33.4 us
    psum x1, blocking collectives, shards(): row_total, target_logit = lax.psum((local_total, target_part), 'vocab')  27.6 us
    all_to_all x1, blocking collectives, shards(): lax.all_to_all(spread, 'seq', split_axis=2, concat_axis=1, tiled=True)  22.6 us
    all_to_all x1, waiting for transfers between devices, shards(): lax.all_to_all(partial_pairs.astype(jnp.bfloat16), 'vocab', split_axis=2,...  15.2 us
    all_gather x1, waiting for transfers between devices, shards(): lax.all_gather(arrived.reshape(2, sequence_count, 1, inner_row_count, HEA...  11.9 us
  transfers between devices with their start and end apart: 8, of which 8 were waited for; matrix products, arithmetic and copies ran while one was open for 4% of the time, Pallas kernels for 0%

commit v1 on v0

v1 whole, which is shorter than its diff:
```python
import jax
import jax.numpy as jnp
from jax import lax
from jax.experimental import pallas as pl
from jax.experimental.pallas import tpu as pltpu
from jax.sharding import PartitionSpec as P

D = 5120
HEAD = 128
SEQ = 32
VOC = 16
TOK = 64
GROUP_HEADS = 3
ROWS = 128
STACK = GROUP_HEADS * ROWS
KEYS = 2048
EPS = 1e-05
LOSS_SCALE = 32.0
MASKED = -1e30
SCALE = HEAD ** (-0.5)
MESH = pl.DeviceIdType.MESH
F32 = jnp.float32
BF16 = jnp.bfloat16


def remote(src, dst, send_sem, recv_sem, **device):
    return pltpu.make_async_remote_copy(
        src_ref=src,
        dst_ref=dst,
        send_sem=send_sem,
        recv_sem=recv_sem,
        device_id=device,
        device_id_type=MESH,
    )


def low_rows(shape):
    return lax.broadcasted_iota(jnp.int32, shape, len(shape) - 2) < 4


def turn(x):
    return pltpu.roll(x, 4, len(x.shape) - 2)


def first_halves(a, b):
    return jnp.where(low_rows(a.shape), a, turn(b))


def second_halves(a, b):
    return jnp.where(low_rows(a.shape), turn(a), b)


def dot_nt(a, b):
    return lax.dot_general(a, b, (((1,), (1,)), ((), ())), preferred_element_type=F32)


def dot_tn(a, b):
    return lax.dot_general(a, b, (((0,), (0,)), ((), ())), preferred_element_type=F32)


def body(
    hidden, gain, weight, targets, out_proj, query, key_value, offset,
    loss_out, hidden_out, query_out, kv_out,
    logits_t, stat_send, stat_recv, part_send, part_recv, gain_chunk, hidden_chunk, grad_pad,
    slice_recv, slice_tiles, blocks, acts, proj_pad, proj_half, proj,
    query_wide, query_send, query_recv, query_rows, kv_send, kv_recv, kv,
    scores, probs_low, prob_grad, score_grad, og,
    dq_send, dq_recv, dkv_send, dkv_recv, fold_send, fold_recv,
    stat_s, stat_r, part_s, part_r, slice_s, slice_r, z_s, z_r, ring_s, ring_r,
    half_s, half_r, proj_s, proj_r, pfwd_s, pfwd_r, q_s, q_r, kv1_s, kv1_r, kv2_s, kv2_r,
    kfwd_s, kfwd_r, dq_s, dq_r, dkv_s, dkv_r, fold_s, fold_r,
):
    s = lax.axis_index("seq")
    v = lax.axis_index("vocab")
    h, y = s // 8, lax.rem(s, 8)
    slot = y * 4 + h
    chip, core = v // 2, lax.rem(v, 2)
    mate = v + 1 - 2 * core

    barrier = pltpu.get_barrier_semaphore()

    @pl.loop(1, VOC)
    def _(d):
        pl.semaphore_signal(
            barrier, inc=1, device_id={"vocab": lax.rem(v + d, VOC)}, device_id_type=MESH
        )

    @pl.loop(1, SEQ)
    def _(d):
        pl.semaphore_signal(
            barrier, inc=1, device_id={"seq": lax.rem(s + d, SEQ)}, device_id_type=MESH
        )

    def square(j, acc):
        x = hidden[:, pl.ds(pl.multiple_of(j * 512, 512), 512)].astype(F32)
        x = x * x
        return acc + (x[:, :128] + x[:, 128:256]) + (x[:, 256:384] + x[:, 384:])

    squares = lax.fori_loop(0, 10, square, jnp.zeros((TOK, 128), F32))
    inv_rms = lax.rsqrt(jnp.sum(squares, axis=1, keepdims=True) / D + EPS)

    def logit_step(j, acc):
        cols = pl.ds(pl.multiple_of(j * 512, 512), 512)
        normed = (hidden[:, cols].astype(F32) * inv_rms * gain[:, cols]).astype(BF16)
        return acc + dot_nt(weight[:, cols], normed)

    logits = lax.fori_loop(0, 10, logit_step, jnp.zeros((256, TOK), F32))
    logits_t[...] = logits
    hit = (v * 256 + lax.broadcasted_iota(jnp.int32, (256, TOK), 0)) == targets[...]
    peak = jnp.max(logits, axis=0, keepdims=True)
    raised = jnp.exp(logits - peak)
    stat_send[...] = jnp.zeros((8, 128), F32)
    stat_send[0:1, 0:TOK] = peak
    stat_send[1:2, 0:TOK] = jnp.sum(raised, axis=0, keepdims=True)
    stat_send[2:3, 0:TOK] = jnp.sum(raised * (logits - peak), axis=0, keepdims=True)
    stat_send[3:4, 0:TOK] = jnp.sum(jnp.where(hit, logits, 0.0), axis=0, keepdims=True)
    stat_recv[v] = stat_send[...]

    query_wide[...] = jnp.zeros(query_wide.shape, F32)
    for t in range(SEQ):
        for j in range(GROUP_HEADS):
            lane = (GROUP_HEADS * t + j) * HEAD
            query_wide[t, 4 * j : 4 * j + 4, :] = query[:, lane : lane + HEAD].astype(F32)
    query_send[...] = query_wide[...].astype(BF16)
    for k in range(8):
        kv_send[k, 0:4, :] = key_value[0, :, k * HEAD : k * HEAD + HEAD].astype(F32)
        kv_send[k, 4:8, :] = key_value[1, :, k * HEAD : k * HEAD + HEAD].astype(F32)
    proj_pad[...] = jnp.zeros(proj_pad.shape, BF16)
    proj_pad[:, 0:320] = out_proj[...]

    pl.semaphore_wait(barrier, VOC - 1 + SEQ - 1)

    def stat_copy(p, q):
        return remote(stat_send, stat_recv.at[q], stat_s.at[p], stat_r.at[q], vocab=p)

    @pl.loop(1, VOC)
    def _(d):
        stat_copy(lax.rem(v + d, VOC), v).start()

    half_copy = remote(
        proj_pad.at[pl.ds(pl.multiple_of(192 * (1 - core), 192), 192)],
        proj_half, half_s, half_r, vocab=mate,
    )
    half_copy.start()

    def kv1_copy(p, where):
        return remote(kv_send.at[p // 4], kv_recv.at[where], kv1_s.at[p], kv1_r.at[where], seq=p)

    def q_copy(p, where):
        return remote(query_send.at[p], query_recv.at[where], q_s.at[p], q_r.at[where], seq=p)

    @pl.loop(1, SEQ)
    def _(d):
        kv1_copy(lax.rem(s + d, SEQ), slot).start()

    @pl.loop(1, SEQ)
    def _(d):
        q_copy(lax.rem(s + d, SEQ), slot).start()

    kv_recv[slot] = kv_send[s // 4]
    query_recv[slot] = query_send[s]

    wide = hidden[pl.ds(pl.multiple_of(16 * (v // 4), 16), 16), :].astype(F32)
    wide = jnp.where(lax.rem(v // 2, 2) == 0, wide[0:8], wide[8:16])
    wide = jnp.where(core == 0, wide, turn(wide))
    gains = jnp.broadcast_to(gain[...], (8, D))

    def own_rows(x):
        x = jnp.broadcast_to(x, (TOK, 128)).reshape(8, 8, 128)
        at = lax.broadcasted_iota(jnp.int32, x.shape, 0) == v // 2
        x = jnp.sum(jnp.where(at, x, 0.0), axis=0)
        x = jnp.where(core == 0, x, turn(x))
        return first_halves(x, x)

    own_inv = own_rows(inv_rms)
    for b in range(20):
        left, right = slice(256 * b, 256 * b + 128), slice(256 * b + 128, 256 * b + 256)
        hidden_chunk[8 * b : 8 * b + 8, :] = first_halves(wide[:, left], wide[:, right])
        gain_chunk[8 * b : 8 * b + 8, :] = own_inv * first_halves(gains[:, left], gains[:, right])

    @pl.loop(1, VOC)
    def _(d):
        stat_copy(v, lax.rem(v + d, VOC)).wait_recv()

    stats = stat_recv[...]
    peaks = stats[:, 0, 0:TOK]
    row_peak = jnp.max(peaks, axis=0, keepdims=True)
    factor = jnp.exp(peaks - row_peak)
    row_total = jnp.sum(stats[:, 1, 0:TOK] * factor, axis=0, keepdims=True)
    weighted = jnp.sum(
        factor * (stats[:, 2, 0:TOK] + stats[:, 1, 0:TOK] * (peaks - row_peak)),
        axis=0, keepdims=True,
    )
    target_logit = jnp.sum(stats[:, 3, 0:TOK], axis=0, keepdims=True)
    loss_out[...] = jnp.log(row_total) + row_peak - target_logit
    tilt = weighted / row_total + (row_peak - target_logit)
    eye = lax.broadcasted_iota(jnp.int32, (TOK, TOK), 0) == lax.broadcasted_iota(
        jnp.int32, (TOK, TOK), 1
    )
    tilt = jnp.sum(jnp.where(eye, jnp.broadcast_to(tilt, (TOK, TOK)), 0.0), axis=1, keepdims=True)
    own_tilt = own_rows(inv_rms * inv_rms * tilt * (LOSS_SCALE / D))

    logits = logits_t[...]
    logit_grad = (
        LOSS_SCALE * (jnp.exp(logits - row_peak) / row_total - hit.astype(F32))
    ).astype(BF16)

    def part_step(j, carry):
        cols = pl.ds(pl.multiple_of(j * 512, 512), 512)
        rows = pl.ds(pl.multiple_of(j * 16, 16), 16)
        out = dot_tn(logit_grad, weight[:, cols])
        t = [out[:, 128 * i : 128 * i + 128].reshape(8, 8, 128) for i in range(4)]
        part_send[:, 0, rows, :] = jnp.concatenate(
            [first_halves(t[0], t[1]), first_halves(t[2], t[3])], axis=1
        ).astype(BF16)
        part_send[:, 1, rows, :] = jnp.concatenate(
            [second_halves(t[0], t[1]), second_halves(t[2], t[3])], axis=1
        ).astype(BF16)
        return carry

    lax.fori_loop(0, 10, part_step, 0)

    def part_copy(p, q):
        return remote(
            part_send.at[p // 2, lax.rem(p, 2)], part_recv.at[q], part_s.at[p], part_r.at[q], vocab=p
        )

    @pl.loop(1, VOC)
    def _(d):
        part_copy(lax.rem(v + d, VOC), v).start()

    part_recv[v] = part_send[chip, core]

    @pl.loop(1, SEQ)
    def _(d):
        o = lax.rem(s + d, SEQ)
        kv1_copy(s, lax.rem(o, 8) * 4 + o // 8).wait_recv()

    pairs = kv_recv[...].reshape(16, 2, 8, 128)
    own_keys = pl.ds(pl.multiple_of(v * ROWS, ROWS), ROWS)
    kv[0, own_keys, :] = first_halves(pairs[:, 0], pairs[:, 1]).reshape(ROWS, 128).astype(BF16)
    kv[1, own_keys, :] = second_halves(pairs[:, 0], pairs[:, 1]).reshape(ROWS, 128).astype(BF16)

    def kv2_copy(c, origin):
        at = kv.at[:, pl.ds(pl.multiple_of((2 * origin + core) * ROWS, ROWS), ROWS), :]
        return remote(at, at, kv2_s.at[c], kv2_r.at[origin], vocab=2 * c + core)

    def kfwd_copy(origin, side):
        at = kv.at[:, pl.ds(pl.multiple_of((2 * origin + side) * ROWS, ROWS), ROWS), :]
        return remote(at, at, kfwd_s.at[origin], kfwd_r.at[origin], vocab=mate)

    @pl.loop(1, 8)
    def _(d):
        kv2_copy(lax.rem(chip + d, 8), chip).start()

    kfwd_copy(chip, core).start()

    half_copy.wait_recv()
    lanes = lax.broadcasted_iota(jnp.int32, (192, 128), 1) < 64
    mine = pl.ds(pl.multiple_of(192 * core, 192), 192)
    lefts, rights = [], []
    for i in range(3):
        a = proj_pad[mine, 128 * i : 128 * i + 128].astype(F32)
        b = proj_half[:, 128 * i : 128 * i + 128].astype(F32)
        lefts.append(jnp.where(core == 0, a, b))
        rights.append(pltpu.roll(jnp.where(core == 0, b, a), 64, 1))
    tiles = [
        lefts[0], lefts[1],
        jnp.where(lanes, lefts[2], rights[0]),
        jnp.where(lanes, rights[0], rights[1]),
        jnp.where(lanes, rights[1], rights[2]),
    ]
    for i in range(5):
        proj[core, :, pl.ds(pl.multiple_of(640 * chip + 128 * i, 128), 128)] = tiles[i].astype(BF16)

    def proj_copy(c, origin):
        at = proj.at[core, :, pl.ds(pl.multiple_of(640 * origin, 640), 640)]
        return remote(at, at, proj_s.at[c], proj_r.at[origin], vocab=2 * c + core)

    def pfwd_copy(origin, side):
        at = proj.at[side, :, pl.ds(pl.multiple_of(640 * origin, 640), 640)]
        return remote(at, at, pfwd_s.at[origin], pfwd_r.at[origin], vocab=mate)

    @pl.loop(1, 8)
    def _(d):
        proj_copy(lax.rem(chip + d, 8), chip).start()

    pfwd_copy(chip, core).start()

    @pl.loop(1, SEQ)
    def _(d):
        o = lax.rem(s + d, SEQ)
        q_copy(s, lax.rem(o, 8) * 4 + o // 8).wait_recv()

    pairs = query_recv[...].astype(F32).reshape(16, 2, 16, 128)
    even, odd = pairs[:, 0], pairs[:, 1]
    query_rows[0:128, :] = first_halves(even[:, 0:8], odd[:, 0:8]).reshape(128, 128).astype(BF16)
    query_rows[128:256, :] = second_halves(even[:, 0:8], odd[:, 0:8]).reshape(128, 128).astype(BF16)
    query_rows[256:384, :] = first_halves(even[:, 8:16], odd[:, 8:16]).reshape(128, 128).astype(BF16)

    @pl.loop(1, VOC)
    def _(d):
        part_copy(v, lax.rem(v + d, VOC)).wait_recv()

    def grad_step(j, carry):
        rows = pl.ds(pl.multiple_of(j * 16, 16), 16)
        total = jnp.sum(part_recv[:, rows, :].astype(F32), axis=0)
        tilt16 = jnp.concatenate([own_tilt, own_tilt], axis=0)
        out = (gain_chunk[rows, :] * total - hidden_chunk[rows, :] * tilt16).astype(BF16)
        grad_pad[rows, :] = out
        blocks[y, h, rows, :] = out
        return carry

    lax.fori_loop(0, 10, grad_step, 0)
    grad_pad[160:176, :] = jnp.zeros((16, 128), BF16)

    def z_copy(d, target, origin):
        return remote(
            blocks.at[y, origin], blocks.at[y, origin], z_s.at[d], z_r.at[d], seq=target * 8 + y
        )

    for d in (1, 3, 2):
        z_copy(d, lax.rem(h + d, 4), h).start()

    def ring_copy(way, k, e, block):
        to = lax.rem(y + 1 + 6 * way, 8)
        at = blocks.at[block, lax.rem(h + e, 4)]
        return remote(at, at, ring_s.at[way, k, e], ring_r.at[way, k, e], seq=h * 8 + to)

    def sent(way, k):
        return lax.rem(y + (8 - k if way == 0 else k), 8)

    def got(way, k):
        return lax.rem(y + (7 - k if way == 0 else k + 1), 8)

    def goes(way, k, e):
        return k < 3 or (e < 2) == (way == 0)

    def first_rows(p):
        return pl.multiple_of((4 * ((5 * p) // 2)) // 16 * 16, 16)

    def slice_copy(p, q):
        return remote(
            grad_pad.at[pl.ds(first_rows(p), 32)], slice_recv.at[q], slice_s.at[p], slice_r.at[q], vocab=p
        )

    for way in range(2):
        ring_copy(way, 0, 0, y).start()

    @pl.loop(1, VOC)
    def _(d):
        slice_copy(lax.rem(v + d, VOC), v).start()

    slice_recv[v] = grad_pad[pl.ds(first_rows(v), 32), :]

    for e in (1, 3, 2):
        z_copy(4 - e, h, lax.rem(h + e, 4)).wait_recv()
        for way in range(2):
            ring_copy(way, 0, e, y).start()

    def ring_step(k):
        for e in (0, 1, 3, 2):
            for way in range(2):
                ring_copy(way, k - 1, e, got(way, k - 1)).wait_recv()
                if goes(way, k, e):
                    ring_copy(way, k, e, sent(way, k)).start()

    @pl.loop(1, 8)
    def _(d):
        o = lax.rem(chip + d, 8)
        kv2_copy(chip, o).wait_recv()
        kfwd_copy(o, core).start()

    @pl.loop(0, 8)
    def _(o):
        kfwd_copy(o, 1 - core).wait_recv()

    ring_step(1)

    start = offset[0]
    r = lax.rem(lax.broadcasted_iota(jnp.int32, (1, STACK), 1), ROWS)
    q_place = (lax.rem(r // 4, 4) * 8 + r // 16) * TOK + 4 * v + lax.rem(r, 4)
    r = lax.broadcasted_iota(jnp.int32, (ROWS, 1), 0)
    k_base = (lax.rem(r // 4, 4) * 8 + r // 16) * TOK + lax.rem(r, 4)
    q_before = q_place < start

    def score_step(c, top):
        keys = pl.ds(pl.multiple_of(c * ROWS, ROWS), ROWS)
        k_place = k_base + 4 * c
        seen = (k_place <= q_place) & ((k_place >= start) | q_before)
        x = jnp.where(seen, dot_nt(kv[0, keys, :], query_rows[...]) * SCALE, MASKED)
        scores[keys, :] = x
        return jnp.maximum(top, jnp.max(x, axis=0, keepdims=True))

    top = lax.fori_loop(0, 16, score_step, jnp.full((1, STACK), MASKED, F32))

    def exp_step(c, total):
        keys = pl.ds(pl.multiple_of(c * ROWS, ROWS), ROWS)
        x = jnp.exp(scores[keys, :] - top)
        scores[keys, :] = x
        return total + jnp.sum(x, axis=0, keepdims=True)

    total = lax.fori_loop(0, 16, exp_step, jnp.zeros((1, STACK), F32))
    share = 1.0 / total

    ring_step(2)

    def prob_step(c, carry):
        keys = pl.ds(pl.multiple_of(c * ROWS, ROWS), ROWS)
        x = scores[keys, :] * share
        scores[keys, :] = x
        probs_low[keys, :] = x.astype(BF16)
        return carry

    lax.fori_loop(0, 16, prob_step, 0)

    ring_step(3)

    @pl.loop(1, 8)
    def _(d):
        o = lax.rem(chip + d, 8)
        proj_copy(chip, o).wait_recv()
        pfwd_copy(o, core).start()

    @pl.loop(1, VOC)
    def _(d):
        slice_copy(v, lax.rem(v + d, VOC)).wait_recv()

    pairs = slice_recv[...].astype(F32).reshape(8, 2, 32, 128)
    for b in range(4):
        even, odd = pairs[:, 0, 8 * b : 8 * b + 8], pairs[:, 1, 8 * b : 8 * b + 8]
        slice_tiles[2 * b] = first_halves(even, odd).reshape(TOK, 128)
        slice_tiles[2 * b + 1] = second_halves(even, odd).reshape(TOK, 128)
    skip = (5 * v) // 2 - first_rows(v) // 4
    lanes = lax.broadcasted_iota(jnp.int32, (TOK, 128), 1) < 64
    t = [slice_tiles[skip + i] for i in range(3)]
    turned = [pltpu.roll(x, 64, 1) for x in t]
    hidden_out[:, 0:128] = jnp.where(
        core == 0, t[0], jnp.where(lanes, turned[0], turned[1])
    ).astype(BF16)
    hidden_out[:, 128:256] = jnp.where(
        core == 0, t[1], jnp.where(lanes, turned[1], turned[2])
    ).astype(BF16)
    hidden_out[:, 256:320] = jnp.where(core == 0, t[2], turned[2])[:, 0:64].astype(BF16)

    for e in range(4):
        way = 0 if e < 2 else 1
        ring_copy(way, 3, e, got(way, 3)).wait_recv()

    def act_step(i, carry):
        b, j = i // 10, lax.rem(i, 10)
        x = blocks[b, :, pl.ds(pl.multiple_of(j * 16, 16), 16), :].astype(F32)
        rows = pl.ds(pl.multiple_of(b * 16, 16), 16)
        for n in range(4):
            part = x[:, 8 * (n // 2) : 8 * (n // 2) + 8]
            join = first_halves if n % 2 == 0 else second_halves
            cols = pl.ds(pl.multiple_of(j * 512 + 128 * n, 128), 128)
            acts[rows, cols] = jnp.concatenate(
                [join(part[0], part[1]), join(part[2], part[3])], axis=0
            ).astype(BF16)
        return carry

    lax.fori_loop(0, 80, act_step, 0)

    @pl.loop(0, 8)
    def _(o):
        pfwd_copy(o, 1 - core).wait_recv()

    for side in range(2):
        out = jnp.zeros((ROWS, 192), F32)

        def og_step(j, acc):
            cols = pl.ds(pl.multiple_of(j * 512, 512), 512)
            return acc + dot_nt(acts[:, cols], proj[side, :, cols])

        og[side] = lax.fori_loop(0, 10, og_step, out).astype(BF16)
    out_grad = jnp.concatenate(
        [
            og[0, :, 0:128],
            jnp.concatenate([og[0, :, 128:192], og[1, :, 0:64]], axis=1),
            og[1, :, 64:192],
        ],
        axis=0,
    )

    def grad_pass(c, delta):
        keys = pl.ds(pl.multiple_of(c * ROWS, ROWS), ROWS)
        x = dot_nt(kv[1, keys, :], out_grad)
        prob_grad[keys, :] = x
        return delta + jnp.sum(probs_low[keys, :].astype(F32) * x, axis=0, keepdims=True)

    delta = lax.fori_loop(0, 16, grad_pass, jnp.zeros((1, STACK), F32))

    def dkv_copy(p, q):
        return remote(dkv_send.at[p], dkv_recv.at[q], dkv_s.at[p], dkv_r.at[q], vocab=p)

    def key_pass(d, carry):
        c = lax.rem(v + d, VOC)
        keys = pl.ds(pl.multiple_of(c * ROWS, ROWS), ROWS)
        ds_low = (scores[keys, :] * (prob_grad[keys, :] - delta)).astype(BF16)
        score_grad[keys, :] = ds_low
        key_part = jnp.dot(ds_low, query_rows[...], preferred_element_type=F32) * SCALE
        value_part = jnp.dot(probs_low[keys, :], out_grad, preferred_element_type=F32)
        dkv_send[c, 0] = key_part.astype(BF16)
        dkv_send[c, 1] = value_part.astype(BF16)

        @pl.when(d < VOC)
        def _():
            dkv_copy(c, v).start()

        return carry

    lax.fori_loop(1, VOC + 1, key_pass, 0)
    dkv_recv[v] = dkv_send[v]

    dq = dot_tn(score_grad[...], kv[0]) * SCALE
    t0, t1, t2 = [dq[128 * j : 128 * j + 128].reshape(16, 8, 128) for j in range(3)]
    dq_send[:, 0] = jnp.concatenate([first_halves(t0, t1), t2], axis=1).astype(BF16)
    dq_send[:, 1] = jnp.concatenate([second_halves(t0, t1), turn(t2)], axis=1).astype(BF16)

    def dq_copy(p, q):
        at = lax.rem(p, 8) * 4 + p // 8
        return remote(
            dq_send.at[at // 2, lax.rem(at, 2)], dq_recv.at[q], dq_s.at[p], dq_r.at[q], seq=p
        )

    @pl.loop(1, SEQ)
    def _(d):
        dq_copy(lax.rem(s + d, SEQ), s).start()

    dq_recv[s] = dq_send[slot // 2, lax.rem(slot, 2)]

    @pl.loop(1, VOC)
    def _(d):
        dkv_copy(v, lax.rem(v + d, VOC)).wait_recv()

    keys_sum = jnp.sum(dkv_recv[:, 0].astype(F32), axis=0).reshape(16, 8, 128)
    values_sum = jnp.sum(dkv_recv[:, 1].astype(F32), axis=0).reshape(16, 8, 128)
    fold_send[:, 0] = first_halves(keys_sum, values_sum)
    fold_send[:, 1] = second_halves(keys_sum, values_sum)

    def fold_copy(p, q):
        at = lax.rem(p, 8) * 4 + p // 8
        return remote(
            fold_send.at[at // 2, lax.rem(at, 2)], fold_recv.at[q], fold_s.at[p], fold_r.at[q], seq=p
        )

    @pl.loop(1, SEQ)
    def _(d):
        fold_copy(lax.rem(s + d, SEQ), s).start()

    fold_recv[s] = fold_send[slot // 2, lax.rem(slot, 2)]

    @pl.loop(1, SEQ)
    def _(d):
        dq_copy(s, lax.rem(s + d, SEQ)).wait_recv()

    for t in range(SEQ):
        x = dq_recv[t].astype(F32)
        for j in range(GROUP_HEADS):
            lane = (GROUP_HEADS * t + j) * HEAD
            query_out[:, lane : lane + HEAD] = x[4 * j : 4 * j + 4].astype(BF16)

    @pl.loop(1, SEQ)
    def _(d):
        fold_copy(s, lax.rem(s + d, SEQ)).wait_recv()

    for k in range(8):
        x = jnp.sum(fold_recv[4 * k : 4 * k + 4], axis=0)
        kv_out[0, :, k * HEAD : k * HEAD + HEAD] = x[0:4].astype(BF16)
        kv_out[1, :, k * HEAD : k * HEAD + HEAD] = x[4:8].astype(BF16)

    half_copy.wait_send()

    @pl.loop(1, VOC)
    def _(d):
        p = lax.rem(v + d, VOC)
        stat_copy(p, v).wait_send()
        part_copy(p, v).wait_send()
        slice_copy(p, v).wait_send()
        dkv_copy(p, v).wait_send()

    @pl.loop(1, SEQ)
    def _(d):
        p = lax.rem(s + d, SEQ)
        kv1_copy(p, slot).wait_send()
        q_copy(p, slot).wait_send()
        dq_copy(p, s).wait_send()
        fold_copy(p, s).wait_send()

    @pl.loop(1, 8)
    def _(d):
        c = lax.rem(chip + d, 8)
        kv2_copy(c, chip).wait_send()
        proj_copy(c, chip).wait_send()

    @pl.loop(0, 8)
    def _(o):
        kfwd_copy(o, core).wait_send()
        pfwd_copy(o, core).wait_send()

    for d in (1, 3, 2):
        z_copy(d, lax.rem(h + d, 4), h).wait_send()
    for k in range(4):
        for e in range(4):
            for way in range(2):
                if goes(way, k, e):
                    ring_copy(way, k, e, sent(way, k)).wait_send()


def scratch():
    v = pltpu.VMEM
    dma = pltpu.SemaphoreType.DMA
    buffers = [
        v((256, TOK), F32), v((8, 128), F32), v((VOC, 8, 128), F32),
        v((8, 2, 160, 128), BF16), v((VOC, 160, 128), BF16),
        v((160, 128), F32), v((160, 128), F32), v((176, 128), BF16),
        v((VOC, 32, 128), BF16), v((8, TOK, 128), F32),
        v((8, 4, 160, 128), BF16), v((ROWS, D), BF16),
        v((384, 384), BF16), v((192, 384), BF16), v((2, 192, D), BF16),
        v((SEQ, 16, 128), F32), v((SEQ, 16, 128), BF16), v((SEQ, 16, 128), BF16), v((STACK, 128), BF16),
        v((8, 8, 128), F32), v((SEQ, 8, 128), F32), v((2, KEYS, 128), BF16),
        v((KEYS, STACK), F32), v((KEYS, STACK), BF16), v((KEYS, STACK), F32), v((KEYS, STACK), BF16),
        v((2, ROWS, 192), BF16),
        v((16, 2, 16, 128), BF16), v((SEQ, 16, 128), BF16),
        v((VOC, 2, ROWS, 128), BF16), v((VOC, 2, ROWS, 128), BF16),
        v((16, 2, 8, 128), F32), v((SEQ, 8, 128), F32),
    ]
    sizes = [
        (VOC,), (VOC,), (VOC,), (VOC,), (VOC,), (VOC,), (4,), (4,), (2, 4, 4), (2, 4, 4),
        None, None, (8,), (8,), (8,), (8,), (SEQ,), (SEQ,), (SEQ,), (SEQ,), (8,), (8,),
        (8,), (8,), (SEQ,), (SEQ,), (VOC,), (VOC,), (SEQ,), (SEQ,),
    ]
    return buffers + [dma if n is None else dma(n) for n in sizes]


def shards(hidden, norm_gain, head_weight, targets, out_proj, query, saved_key_value, offset):
    vmem = pl.BlockSpec(memory_space=pltpu.VMEM)
    loss, hidden_grad, query_grad, kv_grad = pl.pallas_call(
        body,
        out_shape=(
            jax.ShapeDtypeStruct((1, TOK), F32),
            jax.ShapeDtypeStruct((TOK, 320), BF16),
            jax.ShapeDtypeStruct(query.shape, BF16),
            jax.ShapeDtypeStruct(saved_key_value.shape, BF16),
        ),
        in_specs=[vmem] * 7 + [pl.BlockSpec(memory_space=pltpu.SMEM)],
        out_specs=(vmem,) * 4,
        scratch_shapes=scratch(),
        compiler_params=pltpu.CompilerParams(
            collective_id=0, has_side_effects=True, vmem_limit_bytes=56 * 2**20
        ),
    )(
        hidden, norm_gain.reshape(1, D), head_weight, targets.reshape(1, TOK), out_proj, query,
        saved_key_value, offset,
    )
    return loss.reshape(TOK), hidden_grad, query_grad, kv_grad


def solution(mesh):
    in_specs = (
        P("seq", None),
        P(),
        P("vocab", None),
        P("seq"),
        P("seq", "vocab"),
        P(("seq", "vocab"), None),
        P(None, ("seq", "vocab"), None),
        P(),
    )
    out_specs = (
        P("seq"),
        P("seq", "vocab"),
        P(("seq", "vocab"), None),
        P(None, ("seq", "vocab"), None),
    )
    return jax.shard_map(shards, mesh=mesh, in_specs=in_specs, out_specs=out_specs, check_vma=False)
```

time: 507 us -> 134 us (0.26)
  waiting for transfers between devices: 311 us -> 0 us
  Pallas kernels: 0 us -> 125 us
  blocking collectives: 83.6 us -> 0 us
  matrix products: 30.8 us -> 0 us
  starting transfers between devices: 28.7 us -> 0 us
  other arithmetic: 15.9 us -> 0 us
  local copies, waits for them, and re-layouts: 20.6 us -> 7.33 us
  between operations: 14 us -> 1.29 us
    psum x1 -> x0, waiting for transfers between devices: 127 us -> none  [shards(): lax.psum(partial_grad.astype(jnp.bfloat16), 'vocab').astype(jnp.float32)]
    pallas_call x0 -> x1, Pallas kernels: none -> 125 us  [shards(): pl.pallas_call(body, out_shape=(jax.ShapeDtypeStruct((1, TOK), F32), jax....]
    all_gather x2 -> x0, waiting for transfers between devices: 71.7 us -> none  [the longest x1 59.8 us: shards(): lax.all_gather(hidden_slice, 'seq', axis=0, tiled=True)]
    reduce_scatter x1 -> x0, waiting for transfers between devices: 65.8 us -> none  [shards(): lax.psum_scatter(grouped.astype(jnp.bfloat16), 'vocab', scatter_dimension...]
    all_to_all x4 -> x0, waiting for transfers between devices: 46.5 us -> none  [the longest x1 15.2 us: shards(): lax.all_to_all(partial_pairs.astype(jnp.bfloat16), 'vocab', split_axis=2,...]
    pmax x1 -> x0, blocking collectives: 33.4 us -> none  [shards(): row_peak = lax.pmax(jnp.max(logits, axis=-1), 'vocab')]
    dot_general x21 -> x0, matrix products: 30.8 us -> none  [the longest x3 8.92 us: head_backward(): lax.dot_general(probs_low, out_grad, (((0,), (0,)), ((), ())), preferred_...]
    all_to_all x4 -> x0, starting transfers between devices: 28.6 us -> none  [the longest x1 11.5 us: shards(): lax.all_to_all(outgoing, 'seq', split_axis=0, concat_axis=2, tiled=True)]
  transfers between devices with their start and end apart: 8 -> 0, of which waited for: 8 -> 0; matrix products, arithmetic and copies ran while one was open for 4% -> 0% of each run, Pallas kernels for 0% -> 0%
where the time goes in v1:
time: 134 us; the launch traced here: 133 us
  Pallas kernels  125 us (93%)
  local copies, waits for them, and re-layouts  7.33 us (5%)
    pallas_call x1, Pallas kernels, shards(): pl.pallas_call(body, out_shape=(jax.ShapeDtypeStruct((1, TOK), F32), jax....  125 us
    unnamed x5, local copies, waits for them, and re-layouts  7.33 us

profile of v1, /device:TPU:1, one launch (start us, length us, event | category | flops | bytes accessed | tf_op | source)
XLA Modules:
  0.0 133.2 jit_solution(2624581962739028240)
XLA Ops:
  1.3 1.8 %copy.12.out_proj = bf16[384,320]{1,0:T(8,128)(2,1)} copy(bf16[384,320]{0,1:T(8,128)(2,1)} %param.12) | data formatting | bytes 491520 | tf_op args[4]
  3.1 124.6 %shard_map.111 = (f32[1,64]{1,0:T(1,128)}, bf16[64,320]{1,0:T(8,128)(2,1)}, bf16[4,12288]{1,0:T(4,128)(2,1)}, bf16[2,4,1024]{2,1,0:T(4,128)(2,1)}) custom-call(bf16[64,5120]{1,0:T(8,128)(2,1)} %hidden.1, f32[1,5120]{1,0:T(1,128)} %bitcast.3, bf16[256,5120]{1,0:T(8,128)(2,1)} %weight.1, s32[1,64]{1,0:T(1,128)} %bitcast.4, bf16[384,320]{1,0:T(8,128)(2,1)} %copy.12.out_proj, ...), custom_call_target="tpu_custom_call" | custom-call | tf_op jit(solution)/shard_map/pallas_call | solution.py:639
  127.7 1.2 copy.18
  128.9 1.4 %copy.19 = bf16[64,320]{1,0:T(8,128)(2,1)} copy(bf16[64,320]{1,0:T(8,128)(2,1)} %get-tuple-element.17) | data formatting | bytes 81920
  130.3 1.6 %copy.20 = bf16[4,12288]{1,0:T(4,128)(2,1)} copy(bf16[4,12288]{1,0:T(4,128)(2,1)} %get-tuple-element.18) | data formatting | bytes 196608
  131.9 1.3 copy.21

commit v2 on v1

v2 whole, which is shorter than its diff:
```python
import jax
import jax.numpy as jnp
from jax import lax
from jax.experimental import pallas as pl
from jax.experimental.pallas import tpu as pltpu
from jax.sharding import PartitionSpec as P

D = 5120
HEAD = 128
SEQ = 32
VOC = 16
TOK = 64
GROUP_HEADS = 3
ROWS = 128
STACK = GROUP_HEADS * ROWS
KEYS = 2048
EPS = 1e-05
LOSS_SCALE = 32.0
MASKED = -1e30
VMEM_BYTES = 62 * 2**20
SCALE = HEAD ** (-0.5)
MESH = pl.DeviceIdType.MESH
F32 = jnp.float32
BF16 = jnp.bfloat16


def remote(src, dst, send_sem, recv_sem, **device):
    return pltpu.make_async_remote_copy(
        src_ref=src,
        dst_ref=dst,
        send_sem=send_sem,
        recv_sem=recv_sem,
        device_id=device,
        device_id_type=MESH,
    )


def low_rows(shape):
    return lax.broadcasted_iota(jnp.int32, shape, len(shape) - 2) < 4


def turn(x):
    return pltpu.roll(x, 4, len(x.shape) - 2)


def first_halves(a, b):
    return jnp.where(low_rows(a.shape), a, turn(b))


def second_halves(a, b):
    return jnp.where(low_rows(a.shape), turn(a), b)


def dot_nt(a, b):
    return lax.dot_general(a, b, (((1,), (1,)), ((), ())), preferred_element_type=F32)


def dot_tn(a, b):
    return lax.dot_general(a, b, (((0,), (0,)), ((), ())), preferred_element_type=F32)


def body(
    hidden_in, gain_in, weight_in, targets_in, proj_in, query_in, key_value_in, offset,
    loss_res, hidden_res, query_res, kv_res,
    hidden, gain, weight, targets, query, key_value, loss_out, hidden_out, query_out, kv_out,
    logits_t, stat_send, stat_recv, part_send, part_mate, part_sum, part_recv,
    gain_chunk, hidden_chunk, grad_pad, slice_recv, slice_tiles, blocks, acts, proj,
    query_wide, query_send, query_recv, query_rows, kv_send, kv_recv, kv,
    scores, probs_low, prob_grad, score_grad,
    dq_send, dq_recv, dkv_own, dkv_give, dkv_mate, dkv_sum, dkv_recv, fold_send, fold_recv,
    in_s, out_s, stat_s, stat_r, mate_s, mate_r, part_s, part_r, slice_s, slice_r, z_s, z_r, ring_s, ring_r,
    proj_s, proj_z, proj_x, proj_xx, proj_m, q_s, q_r, kv1_s, kv1_r, kv_s, kv_z, kv_x, kv_xx, kvm_s, kvm_r,
    dq_s, dq_r, dkvm_s, dkvm_r, dkv_s, dkv_r, fold_s, fold_r,
):
    s = lax.axis_index("seq")
    v = lax.axis_index("vocab")
    h, y = s // 8, lax.rem(s, 8)
    slot = y * 4 + h
    chip, core = v // 2, lax.rem(v, 2)
    mate = v + 1 - 2 * core
    beside = v + 2 - 4 * lax.rem(chip, 2)

    def around(block, steps):
        return lax.rem(block + 4 * steps, VOC)

    def wait_recv(ref, sem):
        remote(ref, ref, sem, sem, vocab=mate).wait_recv()

    def wait_send(ref, sem):
        remote(ref, ref, sem, sem, vocab=mate).wait_send()

    def proj_rows(block, first=0, count=320):
        return proj.at[pl.ds(pl.multiple_of(320 * block + first, 16), count)]

    loads = [
        pltpu.make_async_copy(src, dst, in_s.at[i])
        for i, (src, dst) in enumerate(
            [
                (hidden_in, hidden), (gain_in, gain), (targets_in, targets),
                (weight_in.at[:, 0:2560], weight.at[:, 0:2560]),
                (weight_in.at[:, 2560:5120], weight.at[:, 2560:5120]),
                (query_in, query), (key_value_in, key_value), (proj_in, proj_rows(v)),
            ]
        )
    ]
    for load in loads:
        load.start()
    barrier = pltpu.get_barrier_semaphore()

    @pl.loop(1, VOC)
    def _(d):
        pl.semaphore_signal(
            barrier, inc=1, device_id={"vocab": lax.rem(v + d, VOC)}, device_id_type=MESH
        )

    @pl.loop(1, SEQ)
    def _(d):
        pl.semaphore_signal(
            barrier, inc=1, device_id={"seq": lax.rem(s + d, SEQ)}, device_id_type=MESH
        )

    stores = [
        pltpu.make_async_copy(src, dst, out_s.at[i])
        for i, (src, dst) in enumerate(
            [(loss_out, loss_res), (hidden_out, hidden_res), (query_out, query_res), (kv_out, kv_res)]
        )
    ]

    def square(j, acc):
        x = hidden[:, pl.ds(pl.multiple_of(j * 512, 512), 512)].astype(F32)
        x = x * x
        return acc + (x[:, :128] + x[:, 128:256]) + (x[:, 256:384] + x[:, 384:])

    loads[0].wait()
    squares = lax.fori_loop(0, 10, square, jnp.zeros((TOK, 128), F32))
    inv_rms = lax.rsqrt(jnp.sum(squares, axis=1, keepdims=True) / D + EPS)
    loads[1].wait()
    loads[3].wait()

    def logit_step(j, acc):
        cols = pl.ds(pl.multiple_of(j * 512, 512), 512)
        normed = (hidden[:, cols].astype(F32) * inv_rms * gain[:, cols]).astype(BF16)
        return acc + dot_nt(weight[:, cols], normed)

    logits = lax.fori_loop(0, 5, logit_step, jnp.zeros((256, TOK), F32))
    loads[4].wait()
    logits = lax.fori_loop(5, 10, logit_step, logits)
    logits_t[...] = logits
    loads[2].wait()
    hit = (v * 256 + lax.broadcasted_iota(jnp.int32, (256, TOK), 0)) == targets[...]
    peak = jnp.max(logits, axis=0, keepdims=True)
    raised = jnp.exp(logits - peak)
    stat_send[...] = jnp.zeros((8, 128), F32)
    stat_send[0:1, 0:TOK] = peak
    stat_send[1:2, 0:TOK] = jnp.sum(raised, axis=0, keepdims=True)
    stat_send[2:3, 0:TOK] = jnp.sum(raised * (logits - peak), axis=0, keepdims=True)
    stat_send[3:4, 0:TOK] = jnp.sum(jnp.where(hit, logits, 0.0), axis=0, keepdims=True)
    stat_recv[v] = stat_send[...]

    for load in loads[5:]:
        load.wait()
    query_wide[...] = jnp.zeros(query_wide.shape, F32)
    for t in range(SEQ):
        for j in range(GROUP_HEADS):
            lane = (GROUP_HEADS * t + j) * HEAD
            query_wide[t, 4 * j : 4 * j + 4, :] = query[:, lane : lane + HEAD].astype(F32)
    query_send[...] = query_wide[...].astype(BF16)
    for k in range(8):
        kv_send[k, 0:4, :] = key_value[0, :, k * HEAD : k * HEAD + HEAD].astype(F32)
        kv_send[k, 4:8, :] = key_value[1, :, k * HEAD : k * HEAD + HEAD].astype(F32)

    pl.semaphore_wait(barrier, VOC - 1 + SEQ - 1)

    @pl.loop(1, VOC)
    def _(d):
        remote(stat_send, stat_recv.at[v], stat_s, stat_r, vocab=lax.rem(v + d, VOC)).start()

    @pl.loop(1, SEQ)
    def _(d):
        p = lax.rem(s + d, SEQ)
        remote(kv_send.at[p // 4], kv_recv.at[slot], kv1_s, kv1_r, seq=p).start()

    def proj_copy(at, sem, to):
        return remote(at, at, proj_s, sem, vocab=to)

    kv_recv[slot] = kv_send[s // 4]
    query_recv[slot] = query_send[s]

    wide = hidden[pl.ds(pl.multiple_of(16 * (v // 4), 16), 16), :].astype(F32)
    wide = jnp.where(lax.rem(v // 2, 2) == 0, wide[0:8], wide[8:16])
    wide = jnp.where(core == 0, wide, turn(wide))
    gains = jnp.broadcast_to(gain[...], (8, D))

    def own_rows(x):
        x = jnp.broadcast_to(x, (TOK, 128)).reshape(8, 8, 128)
        at = lax.broadcasted_iota(jnp.int32, x.shape, 0) == v // 2
        x = jnp.sum(jnp.where(at, x, 0.0), axis=0)
        x = jnp.where(core == 0, x, turn(x))
        return first_halves(x, x)

    own_inv = own_rows(inv_rms)
    for b in range(20):
        left, right = slice(256 * b, 256 * b + 128), slice(256 * b + 128, 256 * b + 256)
        hidden_chunk[8 * b : 8 * b + 8, :] = first_halves(wide[:, left], wide[:, right])
        gain_chunk[8 * b : 8 * b + 8, :] = own_inv * first_halves(gains[:, left], gains[:, right])

    wait_recv(stat_recv.at[pl.ds(0, VOC - 1)], stat_r)
    stats = stat_recv[...]
    peaks = stats[:, 0, 0:TOK]
    row_peak = jnp.max(peaks, axis=0, keepdims=True)
    factor = jnp.exp(peaks - row_peak)
    row_total = jnp.sum(stats[:, 1, 0:TOK] * factor, axis=0, keepdims=True)
    weighted = jnp.sum(
        factor * (stats[:, 2, 0:TOK] + stats[:, 1, 0:TOK] * (peaks - row_peak)),
        axis=0, keepdims=True,
    )
    target_logit = jnp.sum(stats[:, 3, 0:TOK], axis=0, keepdims=True)
    loss_out[...] = jnp.log(row_total) + row_peak - target_logit
    stores[0].start()
    tilt = weighted / row_total + (row_peak - target_logit)
    eye = lax.broadcasted_iota(jnp.int32, (TOK, TOK), 0) == lax.broadcasted_iota(
        jnp.int32, (TOK, TOK), 1
    )
    tilt = jnp.sum(jnp.where(eye, jnp.broadcast_to(tilt, (TOK, TOK)), 0.0), axis=1, keepdims=True)
    own_tilt = own_rows(inv_rms * inv_rms * tilt * (LOSS_SCALE / D))

    logits = logits_t[...]
    logit_grad = (
        LOSS_SCALE * (jnp.exp(logits - row_peak) / row_total - hit.astype(F32))
    ).astype(BF16)

    def part_step(j, carry):
        cols = pl.ds(pl.multiple_of(j * 512, 512), 512)
        rows = pl.ds(pl.multiple_of(j * 16, 16), 16)
        out = dot_tn(logit_grad, weight[:, cols])
        t = [out[:, 128 * i : 128 * i + 128].reshape(8, 8, 128) for i in range(4)]
        part_send[0, :, rows, :] = jnp.concatenate(
            [first_halves(t[0], t[1]), first_halves(t[2], t[3])], axis=1
        ).astype(BF16)
        part_send[1, :, rows, :] = jnp.concatenate(
            [second_halves(t[0], t[1]), second_halves(t[2], t[3])], axis=1
        ).astype(BF16)
        return carry

    halves = [pl.ds(0, 80), pl.ds(80, 80)]

    def mate_copy(i):
        return remote(
            part_send.at[1 - core, :, halves[i]], part_mate.at[:, halves[i]],
            mate_s.at[i], mate_r.at[i], vocab=mate,
        )

    for i in range(2):
        lax.fori_loop(5 * i, 5 * i + 5, part_step, 0)
        mate_copy(i).start()

    for i in range(2):
        mate_copy(i).wait_recv()
        for b in range(5):
            rows = pl.ds(80 * i + 16 * b, 16)
            part_sum[:, rows, :] = (
                part_send[core, :, rows, :].astype(F32) + part_mate[:, rows, :].astype(F32)
            ).astype(BF16)

        @pl.loop(1, 8)
        def _(d):
            m = lax.rem(chip + d, 8)
            remote(
                part_sum.at[m, halves[i]], part_recv.at[chip, halves[i]], part_s, part_r.at[i],
                vocab=2 * m + core,
            ).start()

    @pl.loop(1, SEQ)
    def _(d):
        p = lax.rem(s + d, SEQ)
        remote(query_send.at[p], query_recv.at[slot], q_s, q_r, seq=p).start()

    part_recv[chip] = part_sum[chip]

    wait_recv(kv_recv.at[pl.ds(0, SEQ - 1)], kv1_r)
    pairs = kv_recv[...].reshape(16, 2, 8, 128)
    kv[0, chip, core] = first_halves(pairs[:, 0], pairs[:, 1]).reshape(ROWS, 128).astype(BF16)
    kv[1, chip, core] = second_halves(pairs[:, 0], pairs[:, 1]).reshape(ROWS, 128).astype(BF16)

    def kv_copy(block, sem, to, kinds=slice(0, 2)):
        at = kv.at[kinds, block // 2, lax.rem(block, 2)]
        return remote(at, at, kv_s, sem, vocab=to)

    kv_copy(v, kv_z, beside).start()
    for way in range(2):
        kv_copy(v, kv_x.at[way, 0], around(v, 1 + 2 * way)).start()

    def grad_step(j, carry):
        rows = pl.ds(pl.multiple_of(j * 16, 16), 16)
        total = jnp.sum(part_recv[:, rows, :].astype(F32), axis=0)
        tilt16 = jnp.concatenate([own_tilt, own_tilt], axis=0)
        out = (gain_chunk[rows, :] * total - hidden_chunk[rows, :] * tilt16).astype(BF16)
        grad_pad[rows, :] = out
        blocks[y, h, rows, :] = out
        return carry

    for i in range(2):
        wait_recv(part_recv.at[pl.ds(0, 7), halves[i]], part_r.at[i])
        lax.fori_loop(5 * i, 5 * i + 5, grad_step, 0)
    grad_pad[160:176, :] = jnp.zeros((16, 128), BF16)

    def z_copy(d, target, origin):
        at = blocks.at[y, origin]
        return remote(at, at, z_s, z_r.at[d], seq=target * 8 + y)

    for d in (1, 3, 2):
        z_copy(d, lax.rem(h + d, 4), h).start()

    def ring_copy(way, k, e, block):
        to = lax.rem(y + 1 + 6 * way, 8)
        at = blocks.at[block, lax.rem(h + e, 4)]
        return remote(at, at, ring_s, ring_r.at[way, k, e], seq=h * 8 + to)

    def sent(way, k):
        return lax.rem(y + (8 - k if way == 0 else k), 8)

    def got(way, k):
        return lax.rem(y + (7 - k if way == 0 else k + 1), 8)

    def goes(way, k, e):
        return k < 3 or (e < 2) == (way == 0)

    def first_rows(p):
        return pl.multiple_of((4 * ((5 * p) // 2)) // 16 * 16, 16)

    for way in range(2):
        ring_copy(way, 0, 0, y).start()
    proj_copy(proj_rows(v), proj_z, beside).start()
    for way in range(2):
        proj_copy(proj_rows(v), proj_x.at[way, 0], around(v, 1 + 2 * way)).start()
    proj_copy(proj_rows(v), proj_m, mate).start()

    def proj_next(kind):
        block = v if kind == 0 else beside
        for way in range(2):
            here = around(block, 3 - 2 * way)
            proj_copy(proj_rows(here), proj_x.at[way, kind], mate).wait_recv()
            proj_copy(
                proj_rows(here, 160 * way, 160), proj_xx.at[way, kind], around(v, 1 + 2 * way)
            ).start()
            proj_copy(proj_rows(here), proj_m, mate).start()

    def kv_next(kind):
        block = v if kind == 0 else beside
        for way in range(2):
            here = around(block, 3 - 2 * way)
            kv_copy(here, kv_x.at[way, kind], mate).wait_recv()
            kv_copy(here, kv_xx.at[way, kind], around(v, 1 + 2 * way), slice(way, way + 1)).start()

    def ring_start(e):
        z_copy(4 - e, h, lax.rem(h + e, 4)).wait_recv()
        for way in range(2):
            ring_copy(way, 0, e, y).start()

    def ring_next(k, e):
        for way in range(2):
            if goes(way, k - 1, e):
                ring_copy(way, k - 1, e, got(way, k - 1)).wait_recv()
            if k < 4 and goes(way, k, e):
                ring_copy(way, k, e, sent(way, k)).start()

    kv_copy(beside, kv_z, mate).wait_recv()
    for way in range(2):
        kv_copy(beside, kv_x.at[way, 1], around(v, 1 + 2 * way)).start()
    kv_next(0)
    ring_start(1)
    ring_next(1, 0)
    kv_next(1)
    ring_start(3)
    ring_next(1, 1)
    proj_copy(proj_rows(beside), proj_z, mate).wait_recv()
    for way in range(2):
        proj_copy(proj_rows(beside), proj_x.at[way, 1], around(v, 1 + 2 * way)).start()
    proj_copy(proj_rows(beside), proj_m, mate).start()

    for kind in range(2):
        for way in range(2):
            far = around(v if kind == 0 else beside, 2)
            kv_copy(far, kv_xx.at[way, kind], mate, slice(way, way + 1)).wait_recv()
    remote(kv.at[:, :, core], kv.at[:, :, core], kvm_s, kvm_r, vocab=mate).start()
    ring_next(2, 0)
    ring_start(2)
    ring_next(1, 3)

    @pl.loop(1, VOC)
    def _(d):
        p = lax.rem(v + d, VOC)
        remote(
            grad_pad.at[pl.ds(first_rows(p), 32)], slice_recv.at[v], slice_s, slice_r, vocab=p
        ).start()

    slice_recv[v] = grad_pad[pl.ds(first_rows(v), 32), :]

    wait_recv(query_recv.at[pl.ds(0, SEQ - 1)], q_r)
    pairs = query_recv[...].astype(F32).reshape(16, 2, 16, 128)
    even, odd = pairs[:, 0], pairs[:, 1]
    query_rows[0:128, :] = first_halves(even[:, 0:8], odd[:, 0:8]).reshape(128, 128).astype(BF16)
    query_rows[128:256, :] = second_halves(even[:, 0:8], odd[:, 0:8]).reshape(128, 128).astype(BF16)
    query_rows[256:384, :] = first_halves(even[:, 8:16], odd[:, 8:16]).reshape(128, 128).astype(BF16)

    wait_recv(kv.at[:, :, 1 - core], kvm_r)

    start = offset[0]
    r = lax.rem(lax.broadcasted_iota(jnp.int32, (1, STACK), 1), ROWS)
    q_place = (lax.rem(r // 4, 4) * 8 + r // 16) * TOK + 4 * v + lax.rem(r, 4)
    r = lax.broadcasted_iota(jnp.int32, (256, 1), 0)
    k_base = (lax.rem(r // 4, 4) * 8 + lax.rem(r // 16, 8)) * TOK + 4 * (r // ROWS) + lax.rem(r, 4)
    q_before = q_place < start

    def score_part(m, top):
        keys = slice(256 * m, 256 * m + 256)
        k_place = k_base + 8 * m
        seen = (k_place <= q_place) & ((k_place >= start) | q_before)
        x = dot_nt(kv[0, m].reshape(256, HEAD), query_rows[...]) * SCALE
        x = jnp.where(seen, x, MASKED)
        scores[keys, :] = x
        return jnp.maximum(top, jnp.max(x, axis=0, keepdims=True))

    def exp_part(m, top, total):
        keys = slice(256 * m, 256 * m + 256)
        x = jnp.exp(scores[keys, :] - top)
        scores[keys, :] = x
        return total + jnp.sum(x, axis=0, keepdims=True)

    def prob_part(m, share):
        keys = slice(256 * m, 256 * m + 256)
        x = scores[keys, :] * share
        scores[keys, :] = x
        probs_low[keys, :] = x.astype(BF16)

    state = {"top": jnp.full((1, STACK), MASKED, F32), "total": jnp.zeros((1, STACK), F32)}

    def piece(n):
        if n < 8:
            state["top"] = score_part(n, state["top"])
        elif n < 16:
            state["total"] = exp_part(n - 8, state["top"], state["total"])
        else:
            if n == 16:
                state["share"] = 1.0 / state["total"]
            prob_part(n - 16, state["share"])

    events = [(2, 1), (3, 0), (1, 2), (2, 3), (3, 1), (2, 2), (3, 3), (3, 2), (4, 0)]
    for n in range(24):
        piece(n)
        if n % 2 == 0 and n // 2 < len(events):
            ring_next(*events[n // 2])
        if n == 4:
            proj_next(0)
        if n == 12:
            proj_next(1)

    wait_recv(slice_recv.at[pl.ds(0, VOC - 1)], slice_r)
    pairs = slice_recv[...].astype(F32).reshape(8, 2, 32, 128)
    for b in range(4):
        even, odd = pairs[:, 0, 8 * b : 8 * b + 8], pairs[:, 1, 8 * b : 8 * b + 8]
        slice_tiles[2 * b] = first_halves(even, odd).reshape(TOK, 128)
        slice_tiles[2 * b + 1] = second_halves(even, odd).reshape(TOK, 128)
    skip = (5 * v) // 2 - first_rows(v) // 4
    lanes = lax.broadcasted_iota(jnp.int32, (TOK, 128), 1) < 64
    t = [slice_tiles[skip + i] for i in range(3)]
    turned = [pltpu.roll(x, 64, 1) for x in t]
    hidden_out[:, 0:128] = jnp.where(
        core == 0, t[0], jnp.where(lanes, turned[0], turned[1])
    ).astype(BF16)
    hidden_out[:, 128:256] = jnp.where(
        core == 0, t[1], jnp.where(lanes, turned[1], turned[2])
    ).astype(BF16)
    hidden_out[:, 256:320] = jnp.where(core == 0, t[2], turned[2])[:, 0:64].astype(BF16)
    stores[1].start()

    def act_block(b):
        def act_step(j, carry):
            x = blocks[b, :, pl.ds(pl.multiple_of(j * 16, 16), 16), :].astype(F32)
            rows = pl.ds(pl.multiple_of(b * 16, 16), 16)
            for n in range(4):
                part = x[:, 8 * (n // 2) : 8 * (n // 2) + 8]
                join = first_halves if n % 2 == 0 else second_halves
                cols = pl.ds(pl.multiple_of(j * 512 + 128 * n, 128), 128)
                acts[rows, cols] = jnp.concatenate(
                    [join(part[0], part[1]), join(part[2], part[3])], axis=0
                ).astype(BF16)
            return carry

        lax.fori_loop(0, 10, act_step, 0)

    for d in (0, 1, 2, 3, 5, 6, 7):
        act_block(lax.rem(y + d, 8))

    for kind in range(2):
        far = around(v if kind == 0 else beside, 2)
        for way in range(2):
            proj_copy(proj_rows(far, 160 * way, 160), proj_xx.at[way, kind], mate).wait_recv()
        proj_copy(proj_rows(far), proj_m, mate).start()

    for e in (1, 3, 2):
        ring_next(4, e)
    act_block(lax.rem(y + 4, 8))
    wait_recv(proj.at[pl.ds(0, 2560)], proj_m)

    def og_step(j, acc):
        cols = pl.ds(pl.multiple_of(j * 1024, 1024), 1024)
        return acc + jnp.dot(acts[:, cols], proj[cols, :], preferred_element_type=F32)

    out = lax.fori_loop(0, 5, og_step, jnp.zeros((ROWS, STACK), F32)).astype(BF16)
    out_grad = jnp.concatenate([out[:, 0:128], out[:, 128:256], out[:, 256:384]], axis=0)

    def dkvm_copy(n, m):
        return remote(dkv_give.at[n, m], dkv_mate.at[n, m], dkvm_s, dkvm_r.at[n, m], vocab=mate)

    def share(n, m, part):
        first, second = part[0:128], part[128:256]
        dkv_own[n, m] = jnp.where(core == 0, first, second)
        dkv_give[n, m] = jnp.where(core == 0, second, first).astype(BF16)
        dkvm_copy(n, m).start()

    def pass_on(n, m):
        dkvm_copy(n, m).wait_recv()
        dkv_sum[n, m] = (dkv_own[n, m] + dkv_mate[n, m].astype(F32)).astype(BF16)

    def dkv_copy(n, m):
        return remote(
            dkv_sum.at[n, m], dkv_recv.at[n, chip], dkv_s, dkv_r.at[n], vocab=2 * m + core
        )

    def send_on(n, m):
        pass_on(n, m)
        dkv_copy(n, m).start()

    def value_pass(d, carry):
        m = lax.rem(chip + d, 8)
        keys = pl.ds(pl.multiple_of(m * 256, 256), 256)
        share(1, m, jnp.dot(probs_low[keys, :], out_grad, preferred_element_type=F32))

        @pl.when(d > 4)
        def _():
            send_on(1, lax.rem(chip + d + 4, 8))

        return carry

    lax.fori_loop(1, 9, value_pass, 0)

    delta = jnp.zeros((1, STACK), F32)
    for m in range(4):
        keys = slice(512 * m, 512 * m + 512)
        x = dot_nt(kv[1, 2 * m : 2 * m + 2].reshape(512, HEAD), out_grad)
        prob_grad[keys, :] = x
        delta = delta + jnp.sum(probs_low[keys, :].astype(F32) * x, axis=0, keepdims=True)

    def key_pass(d, carry):
        m = lax.rem(chip + d, 8)
        keys = pl.ds(pl.multiple_of(m * 256, 256), 256)

        @pl.when(d < 4)
        def _():
            send_on(1, lax.rem(chip + d + 4, 8))

        ds_low = (scores[keys, :] * (prob_grad[keys, :] - delta)).astype(BF16)
        score_grad[keys, :] = ds_low
        share(0, m, jnp.dot(ds_low, query_rows[...], preferred_element_type=F32) * SCALE)

        @pl.when(d > 3)
        def _():
            send_on(0, lax.rem(chip + d + 5, 8))

        return carry

    lax.fori_loop(1, 9, key_pass, 0)
    for d in (6, 7):
        send_on(0, lax.rem(chip + d, 8))

    dq = dot_tn(score_grad[...], kv[0].reshape(KEYS, HEAD)) * SCALE
    t0, t1, t2 = [dq[128 * j : 128 * j + 128].reshape(16, 8, 128) for j in range(3)]
    dq_send[:, 0] = jnp.concatenate([first_halves(t0, t1), t2], axis=1).astype(BF16)
    dq_send[:, 1] = jnp.concatenate([second_halves(t0, t1), turn(t2)], axis=1).astype(BF16)

    @pl.loop(1, SEQ)
    def _(d):
        p = lax.rem(s + d, SEQ)
        at = lax.rem(p, 8) * 4 + p // 8
        remote(dq_send.at[at // 2, lax.rem(at, 2)], dq_recv.at[s], dq_s, dq_r, seq=p).start()

    dq_recv[s] = dq_send[slot // 2, lax.rem(slot, 2)]

    for n in range(2):
        pass_on(n, chip)
        dkv_recv[n, chip] = dkv_sum[n, chip]
    wait_recv(dkv_recv.at[1, pl.ds(0, 7)], dkv_r.at[1])
    values_sum = jnp.sum(dkv_recv[1].astype(F32), axis=0).reshape(16, 8, 128)
    wait_recv(dkv_recv.at[0, pl.ds(0, 7)], dkv_r.at[0])
    keys_sum = jnp.sum(dkv_recv[0].astype(F32), axis=0).reshape(16, 8, 128)
    fold_send[:, 0] = first_halves(keys_sum, values_sum)
    fold_send[:, 1] = second_halves(keys_sum, values_sum)

    @pl.loop(1, SEQ)
    def _(d):
        p = lax.rem(s + d, SEQ)
        at = lax.rem(p, 8) * 4 + p // 8
        remote(fold_send.at[at // 2, lax.rem(at, 2)], fold_recv.at[s], fold_s, fold_r, seq=p).start()

    fold_recv[s] = fold_send[slot // 2, lax.rem(slot, 2)]

    wait_send(stat_recv.at[pl.ds(0, VOC - 1)], stat_s)
    for i in range(2):
        mate_copy(i).wait_send()
    wait_send(part_recv.at[pl.ds(0, 7)], part_s)
    wait_send(slice_recv.at[pl.ds(0, VOC - 1)], slice_s)
    wait_send(kv_recv.at[pl.ds(0, SEQ - 1)], kv1_s)
    wait_send(query_recv.at[pl.ds(0, SEQ - 1)], q_s)
    wait_send(kv.at[:, pl.ds(0, 7), 0], kv_s)
    wait_send(kv.at[:, :, core], kvm_s)
    wait_send(proj.at[pl.ds(0, 15 * 320)], proj_s)
    wait_send(blocks.at[0, pl.ds(0, 3)], z_s)
    wait_send(blocks.at[pl.ds(0, 7)], ring_s)
    wait_send(dkv_mate, dkvm_s)
    wait_send(dkv_recv.at[:, pl.ds(0, 7)], dkv_s)
    wait_send(dq_recv.at[pl.ds(0, SEQ - 1)], dq_s)

    wait_recv(dq_recv.at[pl.ds(0, SEQ - 1)], dq_r)
    for t in range(SEQ):
        x = dq_recv[t].astype(F32)
        for j in range(GROUP_HEADS):
            lane = (GROUP_HEADS * t + j) * HEAD
            query_out[:, lane : lane + HEAD] = x[4 * j : 4 * j + 4].astype(BF16)
    stores[2].start()

    wait_send(fold_recv.at[pl.ds(0, SEQ - 1)], fold_s)
    wait_recv(fold_recv.at[pl.ds(0, SEQ - 1)], fold_r)
    for k in range(8):
        x = jnp.sum(fold_recv[4 * k : 4 * k + 4], axis=0)
        kv_out[0, :, k * HEAD : k * HEAD + HEAD] = x[0:4].astype(BF16)
        kv_out[1, :, k * HEAD : k * HEAD + HEAD] = x[4:8].astype(BF16)
    stores[3].start()
    for copy in stores:
        copy.wait()


def scratch():
    v = pltpu.VMEM
    dma = pltpu.SemaphoreType.DMA
    buffers = [
        v((TOK, D), BF16), v((1, D), F32), v((256, D), BF16), v((1, TOK), jnp.int32),
        v((4, 12288), BF16), v((2, 4, 1024), BF16),
        v((1, TOK), F32), v((TOK, 320), BF16), v((4, 12288), BF16), v((2, 4, 1024), BF16),
        v((256, TOK), F32), v((8, 128), F32), v((VOC, 8, 128), F32),
        v((2, 8, 160, 128), BF16), v((8, 160, 128), BF16), v((8, 160, 128), BF16), v((8, 160, 128), BF16),
        v((160, 128), F32), v((160, 128), F32), v((176, 128), BF16),
        v((VOC, 32, 128), BF16), v((8, TOK, 128), F32),
        v((8, 4, 160, 128), BF16), v((ROWS, D), BF16), v((D, STACK), BF16),
        v((SEQ, 16, 128), F32), v((SEQ, 16, 128), BF16), v((SEQ, 16, 128), BF16), v((STACK, 128), BF16),
        v((8, 8, 128), F32), v((SEQ, 8, 128), F32), v((2, 8, 2, ROWS, 128), BF16),
        v((KEYS, STACK), F32), v((KEYS, STACK), BF16), v((KEYS, STACK), F32), v((KEYS, STACK), BF16),
        v((16, 2, 16, 128), BF16), v((SEQ, 16, 128), BF16),
        v((2, 8, ROWS, 128), F32), v((2, 8, ROWS, 128), BF16), v((2, 8, ROWS, 128), BF16),
        v((2, 8, ROWS, 128), BF16), v((2, 8, ROWS, 128), BF16),
        v((16, 2, 8, 128), F32), v((SEQ, 8, 128), F32),
    ]
    sizes = [
        (8,), (4,), None, None, (2,), (2,), None, (2,), None, None, None, (4,), None, (2, 4, 4),
        None, None, (2, 2), (2, 2), None, None, None, None, None, None, None, (2, 2), (2, 2), None, None,
        None, None, None, (2, 8), None, (2,), None, None,
    ]
    return buffers + [dma if n is None else dma(n) for n in sizes]


def store(*refs):
    sems = refs[12]
    for first, second in ((0, 8), (8, 4)):
        copies = [pltpu.make_async_copy(refs[first + i], refs[second + i], sems.at[i]) for i in range(4)]
        for copy in copies:
            copy.start()
        for copy in copies:
            copy.wait()


def shards(hidden, norm_gain, head_weight, targets, out_proj, query, saved_key_value, offset):
    hbm = pl.BlockSpec(memory_space=pltpu.HBM)
    outs = (
        jax.ShapeDtypeStruct((1, TOK), F32),
        jax.ShapeDtypeStruct((TOK, 320), BF16),
        jax.ShapeDtypeStruct(query.shape, BF16),
        jax.ShapeDtypeStruct(saved_key_value.shape, BF16),
    )
    results = pl.pallas_call(
        body,
        out_shape=outs,
        in_specs=[hbm] * 7 + [pl.BlockSpec(memory_space=pltpu.SMEM)],
        out_specs=(hbm,) * 4,
        scratch_shapes=scratch(),
        compiler_params=pltpu.CompilerParams(
            collective_id=0, has_side_effects=True, vmem_limit_bytes=VMEM_BYTES
        ),
    )(
        hidden, norm_gain.reshape(1, D), head_weight, targets.reshape(1, TOK), out_proj.T, query,
        saved_key_value, offset,
    )
    loss, hidden_grad, query_grad, kv_grad = pl.pallas_call(
        store,
        out_shape=outs,
        in_specs=[hbm] * 4,
        out_specs=(hbm,) * 4,
        scratch_shapes=[pltpu.VMEM(x.shape, x.dtype) for x in outs] + [pltpu.SemaphoreType.DMA((4,))],
        compiler_params=pltpu.CompilerParams(vmem_limit_bytes=VMEM_BYTES),
    )(*results)
    return loss.reshape(TOK), hidden_grad, query_grad, kv_grad


def solution(mesh):
    in_specs = (
        P("seq", None),
        P(),
        P("vocab", None),
        P("seq"),
        P("seq", "vocab"),
        P(("seq", "vocab"), None),
        P(None, ("seq", "vocab"), None),
        P(),
    )
    out_specs = (
        P("seq"),
        P("seq", "vocab"),
        P(("seq", "vocab"), None),
        P(None, ("seq", "vocab"), None),
    )
    return jax.shard_map(shards, mesh=mesh, in_specs=in_specs, out_specs=out_specs, check_vma=False)
```

time: 134 us -> 85.7 us (0.64)
  Pallas kernels: 125 us -> 83.5 us
  local copies, waits for them, and re-layouts: 7.33 us -> 0 us
    pallas_call x1 -> x2, Pallas kernels: 125 us -> 83.5 us  [the longest x1 81.9 us: shards(): pl.pallas_call(body, out_shape=outs, in_specs=[hbm] * 7 + [pl.BlockSpec(m...]
    unnamed x5 -> x0, local copies, waits for them, and re-layouts: 7.33 us -> none
where the time goes in v2:
time: 85.7 us; the launch traced here: 84.8 us
  Pallas kernels  83.5 us (97%)
  between operations  1.29 us (2%)
    pallas_call x1, Pallas kernels, shards(): pl.pallas_call(body, out_shape=outs, in_specs=[hbm] * 7 + [pl.BlockSpec(m...  81.9 us

profile of v2, /device:TPU:1, one launch (start us, length us, event | category | flops | bytes accessed | tf_op | source)
XLA Modules:
  0.0 84.8 jit_solution(1919453868536340775)
XLA Ops:
  1.3 81.9 %shard_map.111 = (f32[1,64]{1,0:T(1,128)}, bf16[64,320]{1,0:T(8,128)(2,1)}, bf16[4,12288]{1,0:T(4,128)(2,1)}, bf16[2,4,1024]{2,1,0:T(4,128)(2,1)}) custom-call(bf16[64,5120]{1,0:T(8,128)(2,1)} %hidden_in.1, f32[1,5120]{1,0:T(1,128)} %bitcast.5, bf16[256,5120]{1,0:T(8,128)(2,1)} %weight_in.1, s32[1,64]{1,0:T(1,128)} %bitcast.6, bf16[320,384]{1,0:T(8,128)(2,1)} %bitcast.4, ...), custom_call_target="tpu_custom_call" | custom-call | tf_op jit(solution)/shard_map/pallas_call | solution.py:689
  83.1 1.6 %shard_map.112 = (f32[1,64]{1,0:T(1,128)}, bf16[64,320]{1,0:T(8,128)(2,1)}, bf16[4,12288]{1,0:T(4,128)(2,1)}, bf16[2,4,1024]{2,1,0:T(4,128)(2,1)}) custom-call(f32[1,64]{1,0:T(1,128)} %get-tuple-element.12.refs_0_, bf16[64,320]{1,0:T(8,128)(2,1)} %get-tuple-element.13.refs_1_, bf16[4,12288]{1,0:T(4,128)(2,1)} %get-tuple-element.14.refs_2_, ...), custom_call_target="tpu_custom_call" | custom-call | tf_op jit(solution)/shard_map/pallas_call | solution.py:702

commit v3 on v2

v3 whole, which is shorter than its diff:
```python
import jax
import jax.numpy as jnp
from jax import lax
from jax.experimental import pallas as pl
from jax.experimental.pallas import tpu as pltpu
from jax.sharding import PartitionSpec as P

D = 5120
HEAD = 128
SEQ = 32
VOC = 16
TOK = 64
GROUP_HEADS = 3
ROWS = 128
STACK = GROUP_HEADS * ROWS
KEYS = 2048
EPS = 1e-05
LOSS_SCALE = 32.0
MASKED = -1e30
VMEM_BYTES = 62 * 2**20
SCALE = HEAD ** (-0.5)
MESH = pl.DeviceIdType.MESH
F32 = jnp.float32
BF16 = jnp.bfloat16


def remote(src, dst, send_sem, recv_sem, **device):
    return pltpu.make_async_remote_copy(
        src_ref=src,
        dst_ref=dst,
        send_sem=send_sem,
        recv_sem=recv_sem,
        device_id=device,
        device_id_type=MESH,
    )


def low_rows(shape):
    return lax.broadcasted_iota(jnp.int32, shape, len(shape) - 2) < 4


def turn(x):
    return pltpu.roll(x, 4, len(x.shape) - 2)


def first_halves(a, b):
    return jnp.where(low_rows(a.shape), a, turn(b))


def second_halves(a, b):
    return jnp.where(low_rows(a.shape), turn(a), b)


def dot_nt(a, b):
    return lax.dot_general(a, b, (((1,), (1,)), ((), ())), preferred_element_type=F32)


def dot_tn(a, b):
    return lax.dot_general(a, b, (((0,), (0,)), ((), ())), preferred_element_type=F32)


def body(
    hidden_in, gain_in, weight_in, targets_in, proj_in, query_in, key_value_in, offset,
    loss_res, hidden_res, query_res, kv_res,
    hidden, gain, weight, targets, query, key_value, loss_out, hidden_out, query_out, kv_out,
    grad_rows, part_raw, stat_send, stat_recv, part_send, part_mate, part_sum, part_recv,
    blocks, proj, proj_ends, og_own, og_give, og_mate, og_sum, og_recv,
    query_wide, query_send, queryz_recv, query_recv, query_rows, kv_wide, kvz_send, kvz_recv, kvy_send, kvy_recv, kv,
    scores, probs_low, prob_grad, score_grad,
    dq_send, dqy_recv, dq_recv, dkv_own, dkv_give, dkv_mate, dkv_sum, dkv_recv, foldy_send, foldy_recv, foldz_send, foldz_recv,
    in_s, out_s, stat_s, stat_r, mate_s, mate_r, part_s, part_r, z_s, z_r, ring_s, ring_r,
    ogm_s, ogm_r, og_s, og_r, qz_s, qz_r, q_s, q_r, kvz_s, kvz_r, kvy_s, kvy_r, kv_s, kv_z, kv_x, kv_xx, kvm_r,
    dqy_s, dqy_r, dq_s, dq_r, dkvm_s, dkvm_r, dkv_s, dkv_r, foldy_s, foldy_r, foldz_s, foldz_r,
):
    s = lax.axis_index("seq")
    v = lax.axis_index("vocab")
    h, y = s // 8, lax.rem(s, 8)
    chip, core = v // 2, lax.rem(v, 2)
    mate = v + 1 - 2 * core
    beside = v + 2 - 4 * lax.rem(chip, 2)

    def around(block, steps):
        return lax.rem(block + 4 * steps, VOC)

    def wait_recv(ref, sem):
        remote(ref, ref, sem, sem, vocab=mate).wait_recv()

    def wait_send(ref, sem):
        remote(ref, ref, sem, sem, vocab=mate).wait_send()

    loads = [
        pltpu.make_async_copy(src, dst, in_s.at[i])
        for i, (src, dst) in enumerate(
            [
                (hidden_in, hidden), (gain_in, gain), (targets_in, targets),
                (weight_in.at[:, 0:2560], weight.at[:, 0:2560]),
                (weight_in.at[:, 2560:5120], weight.at[:, 2560:5120]),
                (query_in, query), (key_value_in, key_value), (proj_in, proj),
            ]
        )
    ]
    for load in loads:
        load.start()
    barrier = pltpu.get_barrier_semaphore()

    def z_peer(d):
        return lax.rem(h + d, 4)

    def y_peer(d):
        return lax.rem(y + d, 8)

    for d in (2, 1, 3):
        pl.semaphore_signal(
            barrier, inc=1, device_id={"seq": z_peer(d) * 8 + y}, device_id_type=MESH
        )
    for d in (4, 3, 5, 2, 6, 1, 7):
        pl.semaphore_signal(
            barrier, inc=1, device_id={"seq": h * 8 + y_peer(d)}, device_id_type=MESH
        )

    @pl.loop(1, VOC)
    def _(d):
        pl.semaphore_signal(
            barrier, inc=1, device_id={"vocab": lax.rem(v + d, VOC)}, device_id_type=MESH
        )

    stores = [
        pltpu.make_async_copy(src, dst, out_s.at[i])
        for i, (src, dst) in enumerate(
            [(loss_out, loss_res), (hidden_out, hidden_res), (query_out, query_res), (kv_out, kv_res)]
        )
    ]

    def square(j, acc):
        x = hidden[:, pl.ds(pl.multiple_of(j * 512, 512), 512)].astype(F32)
        x = x * x
        return acc + (x[:, :128] + x[:, 128:256]) + (x[:, 256:384] + x[:, 384:])

    loads[0].wait()
    squares = lax.fori_loop(0, 10, square, jnp.zeros((TOK, 128), F32))
    inv_rms = lax.rsqrt(jnp.sum(squares, axis=1, keepdims=True) / D + EPS)
    loads[1].wait()
    loads[3].wait()

    def logit_step(j, acc):
        cols = pl.ds(pl.multiple_of(j * 1280, 1280), 1280)
        normed = (hidden[:, cols].astype(F32) * inv_rms * gain[:, cols]).astype(BF16)
        return acc + dot_nt(weight[:, cols], normed)

    logits = lax.fori_loop(0, 2, logit_step, jnp.zeros((256, TOK), F32))
    loads[4].wait()
    logits = lax.fori_loop(2, 4, logit_step, logits)
    loads[2].wait()
    hit = (v * 256 + lax.broadcasted_iota(jnp.int32, (256, TOK), 0)) == targets[...]
    peak = jnp.max(logits, axis=0, keepdims=True)
    raised = jnp.exp(logits - peak)
    stat_send[...] = jnp.zeros((8, 128), F32)
    stat_send[0:1, 0:TOK] = peak
    stat_send[1:2, 0:TOK] = jnp.sum(raised, axis=0, keepdims=True)
    stat_send[2:3, 0:TOK] = jnp.sum(raised * (logits - peak), axis=0, keepdims=True)
    stat_send[3:4, 0:TOK] = jnp.sum(jnp.where(hit, logits, 0.0), axis=0, keepdims=True)
    stat_recv[v] = stat_send[...]
    grad_rows[:, 0:TOK] = raised.astype(BF16)
    grad_rows[:, TOK : 2 * TOK] = hit.astype(F32).astype(BF16)

    for load in loads[5:]:
        load.wait()
    query_wide[...] = jnp.zeros(query_wide.shape, F32)
    for t in range(SEQ):
        for j in range(GROUP_HEADS):
            lane = (GROUP_HEADS * t + j) * HEAD
            query_wide[t, 4 * j : 4 * j + 4, :] = query[:, lane : lane + HEAD].astype(F32)
    query_send[...] = query_wide[...].astype(BF16).reshape(query_send.shape)
    for k in range(8):
        kv_wide[k // 2, 8 * (k % 2) : 8 * (k % 2) + 4, :] = key_value[
            0, :, k * HEAD : k * HEAD + HEAD
        ].astype(F32)
        kv_wide[k // 2, 8 * (k % 2) + 4 : 8 * (k % 2) + 8, :] = key_value[
            1, :, k * HEAD : k * HEAD + HEAD
        ].astype(F32)
    kvz_send[...] = kv_wide[...].astype(BF16)

    pl.semaphore_wait(barrier, 3 + 7 + VOC - 1)

    @pl.loop(1, VOC)
    def _(d):
        remote(stat_send, stat_recv.at[v], stat_s, stat_r, vocab=lax.rem(v + d, VOC)).start()

    for d in (1, 3, 2):
        remote(
            kvz_send.at[z_peer(d)], kvz_recv.at[h], kvz_s, kvz_r, seq=z_peer(d) * 8 + y
        ).start()
    kvz_recv[h] = kvz_send[h]

    proj_ends[...] = jnp.zeros(proj_ends.shape, BF16)
    proj_ends[0, 0:64, :] = proj[256:320, :]
    proj_ends[1, 64:128, :] = proj[256:320, :]
    left = lax.broadcasted_iota(jnp.int32, (1, 128), 1) < 64

    def half_turn(x):
        return pltpu.roll(x, 64, 1)

    def shifted(a, b, c):
        a, b, c = half_turn(a), half_turn(b), half_turn(c)
        return jnp.where(left, a, b), jnp.where(left, b, c), c

    def packed(a, b, c):
        return jnp.concatenate([a, b, jnp.where(left, c[0:32], half_turn(c[32:64]))], axis=0)

    def own_columns(ref):
        first = 128 * ((5 * v) // 2)
        t = [
            ref[:, pl.ds(pl.multiple_of(first + 128 * i, 128), 128)].astype(F32) for i in range(3)
        ]
        t = [jnp.broadcast_to(x, (TOK, 128)) for x in t]
        return [jnp.where(core == 0, a, b) for a, b in zip(t, shifted(*t))]

    def raw_step(j, carry):
        cols = pl.ds(pl.multiple_of(j * 1280, 1280), 1280)
        part_raw[:, cols] = dot_tn(grad_rows[...], weight[:, cols])
        return carry

    lax.fori_loop(0, 4, raw_step, 0)
    wait_recv(stat_recv.at[pl.ds(0, VOC - 1)], stat_r)
    stats = stat_recv[...]
    peaks = stats[:, 0, 0:TOK]
    row_peak = jnp.max(peaks, axis=0, keepdims=True)
    factor = jnp.exp(peaks - row_peak)
    row_total = jnp.sum(stats[:, 1, 0:TOK] * factor, axis=0, keepdims=True)
    weighted = jnp.sum(
        factor * (stats[:, 2, 0:TOK] + stats[:, 1, 0:TOK] * (peaks - row_peak)),
        axis=0, keepdims=True,
    )
    target_logit = jnp.sum(stats[:, 3, 0:TOK], axis=0, keepdims=True)
    loss_out[...] = jnp.log(row_total) + row_peak - target_logit
    stores[0].start()
    tilt = weighted / row_total + (row_peak - target_logit)
    eye = lax.broadcasted_iota(jnp.int32, (TOK, TOK), 0) == lax.broadcasted_iota(
        jnp.int32, (TOK, TOK), 1
    )

    def column(row):
        return jnp.sum(
            jnp.where(eye, jnp.broadcast_to(row, (TOK, TOK)), 0.0), axis=1, keepdims=True
        )

    tilt = inv_rms * inv_rms * column(tilt) * (LOSS_SCALE / D)
    grad_scale = column(LOSS_SCALE * jnp.exp(peak - row_peak) / row_total)

    wait_recv(kvz_recv.at[pl.ds(0, 3)], kvz_r)
    both = kvz_recv[...].astype(F32).reshape(4, 2, 8, 128)
    for i in range(2):
        kvy_send[i] = both[:, i].reshape(32, 128).astype(BF16)
    for d in (4, 3, 5, 2, 6, 1, 7):
        remote(
            kvy_send.at[y_peer(d) // 4], kvy_recv.at[y], kvy_s, kvy_r, seq=h * 8 + y_peer(d)
        ).start()
    kvy_recv[y] = kvy_send[y // 4]
    for d in (2, 1, 3):
        remote(
            query_send.at[z_peer(d)], queryz_recv.at[h], qz_s, qz_r, seq=z_peer(d) * 8 + y
        ).start()
    queryz_recv[h] = query_send[h]

    def part_chip(j):
        return 2 * lax.rem(chip // 2 + 1 + j // 2, 4) + lax.rem(j, 2)

    def part_step(j, carry):
        cols = pl.ds(pl.multiple_of(part_chip(2 * j) * 640, 1280), 1280)
        out = grad_scale * part_raw[0:TOK, cols] - LOSS_SCALE * part_raw[TOK : 2 * TOK, cols]
        t = [out[:, 128 * i : 128 * i + 128] for i in range(10)]
        for i in range(2):
            u = t[5 * i : 5 * i + 5]
            part_send[0, 2 * j + i] = packed(u[0], u[1], u[2]).astype(BF16)
            part_send[1, 2 * j + i] = packed(*shifted(u[2], u[3], u[4])).astype(BF16)
        return carry

    def mate_copy(i):
        half = pl.ds(4 * i, 4)
        return remote(
            part_send.at[1 - core, half], part_mate.at[half], mate_s.at[i], mate_r.at[i], vocab=mate
        )

    for i in range(2):
        lax.fori_loop(2 * i, 2 * i + 2, part_step, 0)
        mate_copy(i).start()

    for i in range(2):
        mate_copy(i).wait_recv()
        for j in range(4 * i, 4 * i + 4):
            part_sum[j] = (part_send[core, j].astype(F32) + part_mate[j].astype(F32)).astype(BF16)

            @pl.when(part_chip(j) != chip)
            def _():
                remote(
                    part_sum.at[j], part_recv.at[chip], part_s, part_r,
                    vocab=2 * part_chip(j) + core,
                ).start()

    part_recv[chip] = part_sum[6 + lax.rem(chip, 2)]

    wait_recv(kvy_recv.at[pl.ds(0, 7)], kvy_r)
    pairs = kvy_recv[...].astype(F32).reshape(16, 2, 8, 128)
    kv[0, chip, core] = first_halves(pairs[:, 0], pairs[:, 1]).reshape(ROWS, 128).astype(BF16)
    kv[1, chip, core] = second_halves(pairs[:, 0], pairs[:, 1]).reshape(ROWS, 128).astype(BF16)

    def kv_copy(block, sem, to, kinds=slice(0, 2)):
        at = kv.at[kinds, block // 2, lax.rem(block, 2)]
        return remote(at, at, kv_s, sem, vocab=to)

    kv_copy(v, kv_z, beside).start()
    for way in range(2):
        kv_copy(v, kv_x.at[way, 0], around(v, 1 + 2 * way)).start()
    kv_copy(v, kvm_r, mate).start()

    wait_recv(queryz_recv.at[pl.ds(0, 3)], qz_r)
    for d in (4, 3, 5, 2, 6, 1, 7):
        remote(
            queryz_recv.at[:, y_peer(d)], query_recv.at[y], q_s, q_r, seq=h * 8 + y_peer(d)
        ).start()
    query_recv[y] = queryz_recv[:, y]

    gains, rows = own_columns(gain), own_columns(hidden)
    wait_recv(part_recv.at[pl.ds(0, 7)], part_r)
    total = jnp.sum(part_recv[...].astype(F32), axis=0)
    ends = total[128:160]
    totals = [total[0:64], total[64:128], jnp.concatenate([ends, half_turn(ends)], axis=0)]
    grads = [inv_rms * g * t - x * tilt for g, t, x in zip(gains, totals, rows)]
    blocks[y, h] = packed(*grads).astype(BF16)

    def z_copy(d, target, origin):
        at = blocks.at[y, origin]
        return remote(at, at, z_s, z_r.at[d], seq=target * 8 + y)

    for d in (1, 3, 2):
        z_copy(d, lax.rem(h + d, 4), h).start()

    def ring_copy(way, k, e, block):
        to = lax.rem(y + 1 + 6 * way, 8)
        at = blocks.at[block, lax.rem(h + e, 4)]
        return remote(at, at, ring_s, ring_r.at[way, k, e], seq=h * 8 + to)

    def sent(way, k):
        return lax.rem(y + (8 - k if way == 0 else k), 8)

    def got(way, k):
        return lax.rem(y + (7 - k if way == 0 else k + 1), 8)

    def goes(way, k, e):
        return k < 3 or (e < 2) == (way == 0)

    for way in range(2):
        ring_copy(way, 0, 0, y).start()

    hidden_out[:, 0:128] = grads[0].astype(BF16)
    hidden_out[:, 128:256] = grads[1].astype(BF16)
    hidden_out[:, 256:320] = grads[2][:, 0:64].astype(BF16)
    stores[1].start()

    def kv_next(kind):
        block = v if kind == 0 else beside
        for way in range(2):
            here = around(block, 3 - 2 * way)
            kv_copy(here, kv_x.at[way, kind], mate).wait_recv()
            kv_copy(here, kv_xx.at[way, kind], around(v, 1 + 2 * way), slice(way, way + 1)).start()
            kv_copy(here, kvm_r, mate).start()

    def kv_last(kind):
        far = around(v if kind == 0 else beside, 2)
        for way in range(2):
            kv_copy(far, kv_xx.at[way, kind], mate, slice(way, way + 1)).wait_recv()
        kv_copy(far, kvm_r, mate).start()

    def ring_start(e):
        z_copy(4 - e, h, lax.rem(h + e, 4)).wait_recv()
        for way in range(2):
            ring_copy(way, 0, e, y).start()

    def ring_next(k, e):
        for way in range(2):
            if goes(way, k - 1, e):
                ring_copy(way, k - 1, e, got(way, k - 1)).wait_recv()
            if k < 4 and goes(way, k, e):
                ring_copy(way, k, e, sent(way, k)).start()

    kv_copy(beside, kv_z, mate).wait_recv()
    for way in range(2):
        kv_copy(beside, kv_x.at[way, 1], around(v, 1 + 2 * way)).start()
    kv_copy(beside, kvm_r, mate).start()
    kv_next(0)
    ring_next(1, 0)
    ring_start(1)
    ring_start(3)
    kv_next(1)
    ring_next(2, 0)
    ring_start(2)
    kv_last(0)

    def og_copy(j, b):
        return remote(og_give.at[b], og_mate.at[b], ogm_s, ogm_r.at[j], vocab=mate)

    def og_block(j, b):
        x = blocks[b]
        out = jnp.dot(x[:, 0:64].reshape(256, 128), proj[0:128, :], preferred_element_type=F32)
        out += jnp.dot(x[:, 64:128].reshape(256, 128), proj[128:256, :], preferred_element_type=F32)
        ends = x[:, 128:160].reshape(128, 128)
        ends = [
            jnp.dot(ends, proj_ends[i], preferred_element_type=F32).reshape(4, 32, STACK)
            for i in range(2)
        ]
        out = out.reshape(4, 64, STACK) + jnp.concatenate(ends, axis=1)
        out = [out[i].reshape(8, 8, STACK) for i in range(4)]
        even = jnp.concatenate([first_halves(out[0], out[1]), first_halves(out[2], out[3])], axis=1)
        odd = jnp.concatenate([second_halves(out[0], out[1]), second_halves(out[2], out[3])], axis=1)
        og_own[b] = jnp.where(core == 0, even, odd)
        og_give[b] = jnp.where(core == 0, odd, even).astype(BF16)
        og_copy(j, b).start()

    def og_pass(j, b):
        og_copy(j, b).wait_recv()
        og_sum[b] = (og_own[b] + og_mate[b].astype(F32)).astype(BF16)

        @pl.loop(1, 8)
        def _(d):
            m = lax.rem(chip + d, 8)
            remote(
                og_sum.at[b, m], og_recv.at[chip, b], og_s, og_r, vocab=2 * m + core
            ).start()

        og_recv[chip, b] = og_sum[b, chip]

    order = [lax.rem(y + d, 8) for d in (0, 7, 1, 6, 2, 5, 3, 4)]

    wait_recv(query_recv.at[pl.ds(0, 7)], q_r)
    pairs = query_recv[...].astype(F32).reshape(16, 2, 16, 128)
    even, odd = pairs[:, 0], pairs[:, 1]
    query_rows[0:128, :] = first_halves(even[:, 0:8], odd[:, 0:8]).reshape(128, 128).astype(BF16)
    query_rows[128:256, :] = second_halves(even[:, 0:8], odd[:, 0:8]).reshape(128, 128).astype(BF16)
    query_rows[256:384, :] = first_halves(even[:, 8:16], odd[:, 8:16]).reshape(128, 128).astype(BF16)

    start = offset[0]
    r = lax.rem(lax.broadcasted_iota(jnp.int32, (1, STACK), 1), ROWS)
    q_place = (lax.rem(r // 4, 4) * 8 + r // 16) * TOK + 4 * v + lax.rem(r, 4)
    r = lax.broadcasted_iota(jnp.int32, (256, 1), 0)
    k_base = (lax.rem(r // 4, 4) * 8 + lax.rem(r // 16, 8)) * TOK + 4 * (r // ROWS) + lax.rem(r, 4)
    q_before = q_place < start

    def score_part(m, top):
        keys = slice(256 * m, 256 * m + 256)
        k_place = k_base + 8 * m
        seen = (k_place <= q_place) & ((k_place >= start) | q_before)
        x = dot_nt(kv[0, m].reshape(256, HEAD), query_rows[...]) * SCALE
        x = jnp.where(seen, x, MASKED)
        scores[keys, :] = x
        return jnp.maximum(top, jnp.max(x, axis=0, keepdims=True))

    def exp_part(m, top, total):
        keys = slice(256 * m, 256 * m + 256)
        x = jnp.exp(scores[keys, :] - top)
        scores[keys, :] = x
        return total + jnp.sum(x, axis=0, keepdims=True)

    def prob_part(m, share):
        keys = slice(256 * m, 256 * m + 256)
        x = scores[keys, :] * share
        scores[keys, :] = x
        probs_low[keys, :] = x.astype(BF16)

    state = {"top": jnp.full((1, STACK), MASKED, F32), "total": jnp.zeros((1, STACK), F32)}

    def piece(n):
        if n < 8:
            state["top"] = score_part(n, state["top"])
        elif n < 16:
            state["total"] = exp_part(n - 8, state["top"], state["total"])
        else:
            if n == 16:
                state["share"] = 1.0 / state["total"]
            prob_part(n - 16, state["share"])

    def pieces(first, last):
        for n in range(first, last):
            piece(n)

    og_block(0, order[0])
    ring_next(1, 1)
    ring_next(1, 3)
    kv_last(1)
    ring_next(3, 0)
    ring_next(1, 2)
    og_block(1, order[1])
    og_block(2, order[2])
    ring_next(2, 1)
    og_pass(0, order[0])
    ring_next(2, 3)
    wait_recv(kv.at[:, :, 1 - core], kvm_r)
    pieces(0, 3)
    ring_next(4, 0)
    ring_next(2, 2)
    og_block(3, order[3])
    og_pass(1, order[1])
    ring_next(3, 1)
    og_block(4, order[4])
    og_pass(2, order[2])
    ring_next(3, 3)
    pieces(3, 7)
    ring_next(3, 2)
    og_block(5, order[5])
    og_pass(3, order[3])
    og_block(6, order[6])
    og_pass(4, order[4])
    ring_next(4, 1)
    ring_next(4, 3)
    pieces(7, 10)
    og_pass(5, order[5])
    ring_next(4, 2)
    og_block(7, order[7])
    og_pass(6, order[6])
    pieces(10, 18)
    og_pass(7, order[7])
    pieces(18, 24)
    wait_recv(og_recv.at[pl.ds(0, 7)], og_r)
    out = jnp.sum(og_recv[...].astype(F32), axis=0).reshape(ROWS, STACK).astype(BF16)
    out_grad = jnp.concatenate([out[:, 0:128], out[:, 128:256], out[:, 256:384]], axis=0)

    def group(j):
        return lax.rem(chip // 2 + 1 + j, 4)

    def group_keys(j):
        return pl.ds(pl.multiple_of(group(j) * 512, 512), 512)

    def dkvm_copy(n, j):
        return remote(dkv_give.at[n, j], dkv_mate.at[n, j], dkvm_s, dkvm_r.at[n, j], vocab=mate)

    def share(n, j, part):
        part = part.reshape(2, 2, ROWS, HEAD)
        first, second = part[:, 0], part[:, 1]
        dkv_own[n, j] = jnp.where(core == 0, first, second)
        dkv_give[n, j] = jnp.where(core == 0, second, first).astype(BF16)
        dkvm_copy(n, j).start()

    def send_on(n, j):
        dkvm_copy(n, j).wait_recv()
        dkv_sum[n, j] = (dkv_own[n, j] + dkv_mate[n, j].astype(F32)).astype(BF16)
        for i in range(2):
            m = 2 * group(j) + i

            @pl.when(m != chip)
            def _():
                remote(
                    dkv_sum.at[n, j, i], dkv_recv.at[n, chip], dkv_s, dkv_r.at[n], vocab=2 * m + core
                ).start()

    def value_pass(j):
        share(1, j, jnp.dot(probs_low[group_keys(j), :], out_grad, preferred_element_type=F32))

    def key_pass(j):
        keys = group_keys(j)
        ds_low = (scores[keys, :] * (prob_grad[keys, :] - delta)).astype(BF16)
        score_grad[keys, :] = ds_low
        share(0, j, jnp.dot(ds_low, query_rows[...], preferred_element_type=F32) * SCALE)

    value_pass(0)
    value_pass(1)
    value_pass(2)
    send_on(1, 0)
    value_pass(3)
    send_on(1, 1)

    delta = jnp.zeros((1, STACK), F32)
    for m in range(4):
        keys = slice(512 * m, 512 * m + 512)
        x = dot_nt(kv[1, 2 * m : 2 * m + 2].reshape(512, HEAD), out_grad)
        prob_grad[keys, :] = x
        delta = delta + jnp.sum(probs_low[keys, :].astype(F32) * x, axis=0, keepdims=True)

    send_on(1, 2)
    send_on(1, 3)
    key_pass(0)
    key_pass(1)
    key_pass(2)
    send_on(0, 0)
    key_pass(3)
    send_on(0, 1)
    send_on(0, 2)

    dq = dot_tn(score_grad[...], kv[0].reshape(KEYS, HEAD)) * SCALE
    send_on(0, 3)
    t0, t1, t2 = [dq[128 * j : 128 * j + 128].reshape(16, 8, 128) for j in range(3)]
    t0 = jnp.concatenate([first_halves(t0, t1), t2, second_halves(t0, t1), turn(t2)], axis=1)
    dq_send[...] = t0.astype(BF16).reshape(dq_send.shape)

    for d in (4, 3, 5, 2, 6, 1, 7):
        remote(
            dq_send.at[y_peer(d)], dqy_recv.at[y], dqy_s, dqy_r, seq=h * 8 + y_peer(d)
        ).start()
    dqy_recv[y] = dq_send[y]

    for n in range(2):
        dkv_recv[n, chip] = dkv_sum[n, 3, lax.rem(chip, 2)]
    wait_recv(dkv_recv.at[1, pl.ds(0, 7)], dkv_r.at[1])
    values_sum = jnp.sum(dkv_recv[1].astype(F32), axis=0).reshape(16, 8, 128)
    wait_recv(dkv_recv.at[0, pl.ds(0, 7)], dkv_r.at[0])
    keys_sum = jnp.sum(dkv_recv[0].astype(F32), axis=0).reshape(16, 8, 128)
    parts = jnp.stack(
        [first_halves(keys_sum, values_sum), second_halves(keys_sum, values_sum)], axis=1
    )
    foldy_send[...] = parts.reshape(8, 32, 128).astype(BF16)
    for d in (4, 3, 5, 2, 6, 1, 7):
        remote(
            foldy_send.at[y_peer(d)], foldy_recv.at[y], foldy_s, foldy_r, seq=h * 8 + y_peer(d)
        ).start()
    foldy_recv[y] = foldy_send[y]

    wait_recv(dqy_recv.at[pl.ds(0, 7)], dqy_r)
    for d in (2, 1, 3):
        remote(
            dqy_recv.at[:, z_peer(d)], dq_recv.at[h], dq_s, dq_r, seq=z_peer(d) * 8 + y
        ).start()
    dq_recv[h] = dqy_recv[:, h]

    wait_send(stat_recv.at[pl.ds(0, VOC - 1)], stat_s)
    for i in range(2):
        mate_copy(i).wait_send()
    wait_send(part_recv.at[pl.ds(0, 7)], part_s)
    wait_send(og_mate, ogm_s)
    wait_send(og_recv.at[pl.ds(0, 7)], og_s)
    wait_send(kvz_recv.at[pl.ds(0, 3)], kvz_s)
    wait_send(kvy_recv.at[pl.ds(0, 7)], kvy_s)
    wait_send(queryz_recv.at[pl.ds(0, 3)], qz_s)
    wait_send(query_recv.at[pl.ds(0, 7)], q_s)
    wait_send(score_grad.at[pl.ds(0, 1280)], kv_s)
    wait_send(blocks.at[0, pl.ds(0, 3)], z_s)
    wait_send(blocks.at[pl.ds(0, 7)], ring_s)
    wait_send(dkv_mate, dkvm_s)
    wait_send(dkv_recv.at[:, pl.ds(0, 7)], dkv_s)
    wait_send(dqy_recv.at[pl.ds(0, 7)], dqy_s)

    def dq_out():
        wait_recv(dq_recv.at[pl.ds(0, 3)], dq_r)
        for t in range(SEQ):
            x = dq_recv[t // 8, t % 8].astype(F32)
            for j in range(GROUP_HEADS):
                lane = (GROUP_HEADS * t + j) * HEAD
                query_out[:, lane : lane + HEAD] = x[4 * j : 4 * j + 4].astype(BF16)
        stores[2].start()

    wait_recv(foldy_recv.at[pl.ds(0, 7)], foldy_r)
    sums = []
    for i in range(2):
        head_sum = jnp.sum(foldy_recv[4 * i : 4 * i + 4].astype(F32), axis=0)
        sums.append(head_sum.reshape(4, 8, 128))
    foldz_send[...] = jnp.concatenate(sums, axis=1).astype(BF16)
    for d in (2, 1, 3):
        remote(
            foldz_send.at[z_peer(d)], foldz_recv.at[h], foldz_s, foldz_r, seq=z_peer(d) * 8 + y
        ).start()
    foldz_recv[h] = foldz_send[h]
    dq_out()
    wait_send(dq_recv.at[pl.ds(0, 3)], dq_s)
    wait_send(foldy_recv.at[pl.ds(0, 7)], foldy_s)
    wait_send(foldz_recv.at[pl.ds(0, 3)], foldz_s)
    wait_recv(foldz_recv.at[pl.ds(0, 3)], foldz_r)
    for k in range(8):
        x = foldz_recv[k // 2].astype(F32)[8 * (k % 2) : 8 * (k % 2) + 8]
        kv_out[0, :, k * HEAD : k * HEAD + HEAD] = x[0:4].astype(BF16)
        kv_out[1, :, k * HEAD : k * HEAD + HEAD] = x[4:8].astype(BF16)
    stores[3].start()
    for copy in stores:
        copy.wait()


def scratch():
    v = pltpu.VMEM
    dma = pltpu.SemaphoreType.DMA
    buffers = [
        v((TOK, D), BF16), v((1, D), F32), v((256, D), BF16), v((1, TOK), jnp.int32),
        v((4, 12288), BF16), v((2, 4, 1024), BF16),
        v((1, TOK), F32), v((TOK, 320), BF16), v((4, 12288), BF16), v((2, 4, 1024), BF16),
        v((256, 2 * TOK), BF16), v((2 * TOK, D), F32), v((8, 128), F32), v((VOC, 8, 128), F32),
        v((2, 8, 160, 128), BF16), v((8, 160, 128), BF16), v((8, 160, 128), BF16), v((8, 160, 128), BF16),
        v((8, 4, 160, 128), BF16), v((320, STACK), BF16), v((2, 128, STACK), BF16),
        v((8, 8, 16, STACK), F32), v((8, 8, 16, STACK), BF16), v((8, 8, 16, STACK), BF16),
        v((8, 8, 16, STACK), BF16), v((8, 8, 16, STACK), BF16),
        v((SEQ, 16, 128), F32), v((4, 8, 16, 128), BF16), v((4, 8, 16, 128), BF16), v((8, 4, 16, 128), BF16),
        v((STACK, 128), BF16),
        v((4, 16, 128), F32), v((4, 16, 128), BF16), v((4, 16, 128), BF16),
        v((2, 32, 128), BF16), v((8, 32, 128), BF16), v((2, 8, 2, ROWS, 128), BF16),
        v((KEYS, STACK), F32), v((KEYS, STACK), BF16), v((KEYS, STACK), F32), v((KEYS, STACK), BF16),
        v((8, 4, 16, 128), BF16), v((8, 4, 16, 128), BF16), v((4, 8, 16, 128), BF16),
        v((2, 4, 2, ROWS, 128), F32), v((2, 4, 2, ROWS, 128), BF16), v((2, 4, 2, ROWS, 128), BF16),
        v((2, 4, 2, ROWS, 128), BF16), v((2, 8, ROWS, 128), BF16),
        v((8, 32, 128), BF16), v((8, 32, 128), BF16), v((4, 16, 128), BF16), v((4, 16, 128), BF16),
    ]
    sizes = [
        (8,), (4,), None, None, (2,), (2,), None, None, None, (4,), None, (2, 4, 4),
        None, (8,), None, None, None, None, None, None, None, None, None, None,
        None, None, (2, 2), (2, 2), None,
        None, None, None, None, None, (2, 4), None, (2,), None, None, None, None,
    ]
    return buffers + [dma if n is None else dma(n) for n in sizes]


def store(*refs):
    sems = refs[12]
    for first, second in ((0, 8), (8, 4)):
        copies = [pltpu.make_async_copy(refs[first + i], refs[second + i], sems.at[i]) for i in range(4)]
        for copy in copies:
            copy.start()
        for copy in copies:
            copy.wait()


def shards(hidden, norm_gain, head_weight, targets, out_proj, query, saved_key_value, offset):
    hbm = pl.BlockSpec(memory_space=pltpu.HBM)
    outs = (
        jax.ShapeDtypeStruct((1, TOK), F32),
        jax.ShapeDtypeStruct((TOK, 320), BF16),
        jax.ShapeDtypeStruct(query.shape, BF16),
        jax.ShapeDtypeStruct(saved_key_value.shape, BF16),
    )
    results = pl.pallas_call(
        body,
        out_shape=outs,
        in_specs=[hbm] * 7 + [pl.BlockSpec(memory_space=pltpu.SMEM)],
        out_specs=(hbm,) * 4,
        scratch_shapes=scratch(),
        compiler_params=pltpu.CompilerParams(
            collective_id=0, has_side_effects=True, vmem_limit_bytes=VMEM_BYTES
        ),
    )(
        hidden, norm_gain.reshape(1, D), head_weight, targets.reshape(1, TOK), out_proj.T, query,
        saved_key_value, offset,
    )
    loss, hidden_grad, query_grad, kv_grad = pl.pallas_call(
        store,
        out_shape=outs,
        in_specs=[hbm] * 4,
        out_specs=(hbm,) * 4,
        scratch_shapes=[pltpu.VMEM(x.shape, x.dtype) for x in outs] + [pltpu.SemaphoreType.DMA((4,))],
        compiler_params=pltpu.CompilerParams(vmem_limit_bytes=VMEM_BYTES),
    )(*results)
    return loss.reshape(TOK), hidden_grad, query_grad, kv_grad


def solution(mesh):
    in_specs = (
        P("seq", None),
        P(),
        P("vocab", None),
        P("seq"),
        P("seq", "vocab"),
        P(("seq", "vocab"), None),
        P(None, ("seq", "vocab"), None),
        P(),
    )
    out_specs = (
        P("seq"),
        P("seq", "vocab"),
        P(("seq", "vocab"), None),
        P(None, ("seq", "vocab"), None),
    )
    return jax.shard_map(shards, mesh=mesh, in_specs=in_specs, out_specs=out_specs, check_vma=False)
```

time: 85.7 us -> 77.3 us (0.902)
  Pallas kernels: 83.5 us -> 75.9 us
    pallas_call x1, Pallas kernels: 81.9 us -> 74.2 us  [shards(): pl.pallas_call(body, out_shape=outs, in_specs=[hbm] * 7 + [pl.BlockSpec(m...]
where the time goes in v3:
time: 77.3 us; the launch traced here: 77.1 us
  Pallas kernels  75.9 us (98%)
  between operations  1.29 us (2%)
    pallas_call x1, Pallas kernels, shards(): pl.pallas_call(body, out_shape=outs, in_specs=[hbm] * 7 + [pl.BlockSpec(m...  74.2 us
    pallas_call x1, Pallas kernels, shards(): pl.pallas_call(store, out_shape=outs, in_specs=[hbm] * 4, out_specs=(hbm,...  1.62 us

profile of v3, /device:TPU:1, one launch (start us, length us, event | category | flops | bytes accessed | tf_op | source)
XLA Modules:
  0.0 77.1 jit_solution(3872090609410384510)
XLA Ops:
  1.3 74.2 %shard_map.111 = (f32[1,64]{1,0:T(1,128)}, bf16[64,320]{1,0:T(8,128)(2,1)}, bf16[4,12288]{1,0:T(4,128)(2,1)}, bf16[2,4,1024]{2,1,0:T(4,128)(2,1)}) custom-call(bf16[64,5120]{1,0:T(8,128)(2,1)} %hidden_in.1, f32[1,5120]{1,0:T(1,128)} %bitcast.5, bf16[256,5120]{1,0:T(8,128)(2,1)} %weight_in.1, s32[1,64]{1,0:T(1,128)} %bitcast.6, bf16[320,384]{1,0:T(8,128)(2,1)} %bitcast.4, ...), custom_call_target="tpu_custom_call" | custom-call | tf_op jit(solution)/shard_map/pallas_call | solution.py:722
  75.5 1.6 %shard_map.112 = (f32[1,64]{1,0:T(1,128)}, bf16[64,320]{1,0:T(8,128)(2,1)}, bf16[4,12288]{1,0:T(4,128)(2,1)}, bf16[2,4,1024]{2,1,0:T(4,128)(2,1)}) custom-call(f32[1,64]{1,0:T(1,128)} %get-tuple-element.12.refs_0_, bf16[64,320]{1,0:T(8,128)(2,1)} %get-tuple-element.13.refs_1_, bf16[4,12288]{1,0:T(4,128)(2,1)} %get-tuple-element.14.refs_2_, ...), custom_call_target="tpu_custom_call" | custom-call | tf_op jit(solution)/shard_map/pallas_call | solution.py:735

commit v4 on v3

--- a/solution.py
+++ b/solution.py
@@ -64,12 +64,12 @@
     loss_res, hidden_res, query_res, kv_res,
     hidden, gain, weight, targets, query, key_value, loss_out, hidden_out, query_out, kv_out,
     grad_rows, part_raw, stat_send, stat_recv, part_send, part_mate, part_sum, part_recv,
-    blocks, proj, proj_ends, og_own, og_give, og_mate, og_sum, og_recv,
-    query_wide, query_send, queryz_recv, query_recv, query_rows, kv_wide, kvz_send, kvz_recv, kvy_send, kvy_recv, kv,
+    blocks, acts, projs, og_own, og_give, og_mate, og_sum, og_recv, ogy_send, ogy_recv,
+    query_wide, query_send, queryy_recv, query_recv, query_rows, kv_wide, kvz_send, kvz_recv, kvy_send, kvy_recv, kv,
     scores, probs_low, prob_grad, score_grad,
     dq_send, dqy_recv, dq_recv, dkv_own, dkv_give, dkv_mate, dkv_sum, dkv_recv, foldy_send, foldy_recv, foldz_send, foldz_recv,
-    in_s, out_s, stat_s, stat_r, mate_s, mate_r, part_s, part_r, z_s, z_r, ring_s, ring_r,
-    ogm_s, ogm_r, og_s, og_r, qz_s, qz_r, q_s, q_r, kvz_s, kvz_r, kvy_s, kvy_r, kv_s, kv_z, kv_x, kv_xx, kvm_r,
+    in_s, out_s, stat_s, stat_r, mate_s, mate_r, part_s, part_r, z_s, z_r, proj_s, proj_r,
+    ogm_s, ogm_r, og_s, og_r, ogy_s, ogy_r, qy_s, qy_r, q_s, q_r, kvz_s, kvz_r, kvy_s, kvy_r, kv_s, kv_z, kv_x, kv_xx, kvm_r,
     dqy_s, dqy_r, dq_s, dq_r, dkvm_s, dkvm_r, dkv_s, dkv_r, foldy_s, foldy_r, foldz_s, foldz_r,
 ):
     s = lax.axis_index("seq")
@@ -95,7 +95,7 @@
                 (hidden_in, hidden), (gain_in, gain), (targets_in, targets),
                 (weight_in.at[:, 0:2560], weight.at[:, 0:2560]),
                 (weight_in.at[:, 2560:5120], weight.at[:, 2560:5120]),
-                (query_in, query), (key_value_in, key_value), (proj_in, proj),
+                (query_in, query), (key_value_in, key_value), (proj_in, projs.at[y, 0:320]),
             ]
         )
     ]
@@ -169,7 +169,7 @@
     for t in range(SEQ):
         for j in range(GROUP_HEADS):
             lane = (GROUP_HEADS * t + j) * HEAD
-            query_wide[t, 4 * j : 4 * j + 4, :] = query[:, lane : lane + HEAD].astype(F32)
+            query_wide[t % 8 * 4 + t // 8, 4 * j : 4 * j + 4, :] = query[:, lane : lane + HEAD].astype(F32)
     query_send[...] = query_wide[...].astype(BF16).reshape(query_send.shape)
     for k in range(8):
         kv_wide[k // 2, 8 * (k % 2) : 8 * (k % 2) + 4, :] = key_value[
@@ -192,9 +192,30 @@
         ).start()
     kvz_recv[h] = kvz_send[h]
 
-    proj_ends[...] = jnp.zeros(proj_ends.shape, BF16)
-    proj_ends[0, 0:64, :] = proj[256:320, :]
-    proj_ends[1, 64:128, :] = proj[256:320, :]
+    def proj_copy(way, k, f, block):
+        at = projs.at[block, 160 * f : 160 * f + 160]
+        to = lax.rem(y + 1 + 6 * way, 8)
+        return remote(at, at, proj_s, proj_r.at[way, k, f], seq=h * 8 + to)
+
+    def sent(way, k):
+        return lax.rem(y + (8 - k if way == 0 else k), 8)
+
+    def got(way, k):
+        return lax.rem(y + (7 - k if way == 0 else k + 1), 8)
+
+    def goes(way, k, f):
+        return k < 3 or f == way
+
+    def proj_next(k, f):
+        for way in range(2):
+            if k > 0 and goes(way, k - 1, f):
+                proj_copy(way, k - 1, f, got(way, k - 1)).wait_recv()
+            if k < 4 and goes(way, k, f):
+                proj_copy(way, k, f, sent(way, k)).start()
+
+    proj_next(0, 0)
+    proj_next(0, 1)
+
     left = lax.broadcasted_iota(jnp.int32, (1, 128), 1) < 64
 
     def half_turn(x):
@@ -256,12 +277,11 @@
             kvy_send.at[y_peer(d) // 4], kvy_recv.at[y], kvy_s, kvy_r, seq=h * 8 + y_peer(d)
         ).start()
     kvy_recv[y] = kvy_send[y // 4]
-    for d in (2, 1, 3):
+    for d in (4, 3, 5, 2, 6, 1, 7):
         remote(
-            query_send.at[z_peer(d)], queryz_recv.at[h], qz_s, qz_r, seq=z_peer(d) * 8 + y
+            query_send.at[y_peer(d)], queryy_recv.at[y], qy_s, qy_r, seq=h * 8 + y_peer(d)
         ).start()
-    queryz_recv[h] = query_send[h]
-
+    queryy_recv[y] = query_send[y]
     def part_chip(j):
         return 2 * lax.rem(chip // 2 + 1 + j // 2, 4) + lax.rem(j, 2)
 
@@ -285,19 +305,29 @@
         lax.fori_loop(2 * i, 2 * i + 2, part_step, 0)
         mate_copy(i).start()
 
+    portions = [pl.ds(0, 64), pl.ds(64, 96)]
+
+    def part_copy(j, f):
+        @pl.when(part_chip(j) != chip)
+        def _():
+            remote(
+                part_sum.at[j, portions[f]], part_recv.at[chip, portions[f]], part_s, part_r.at[f],
+                vocab=2 * part_chip(j) + core,
+            ).start()
+
     for i in range(2):
         mate_copy(i).wait_recv()
         for j in range(4 * i, 4 * i + 4):
             part_sum[j] = (part_send[core, j].astype(F32) + part_mate[j].astype(F32)).astype(BF16)
 
-            @pl.when(part_chip(j) != chip)
-            def _():
-                remote(
-                    part_sum.at[j], part_recv.at[chip], part_s, part_r,
-                    vocab=2 * part_chip(j) + core,
-                ).start()
-
+            part_copy(j, 0)
+
+    for j in range(8):
+        part_copy(j, 1)
     part_recv[chip] = part_sum[6 + lax.rem(chip, 2)]
+
+    proj_next(1, 0)
+    proj_next(1, 1)
 
     wait_recv(kvy_recv.at[pl.ds(0, 7)], kvy_r)
     pairs = kvy_recv[...].astype(F32).reshape(16, 2, 8, 128)
@@ -313,49 +343,15 @@
         kv_copy(v, kv_x.at[way, 0], around(v, 1 + 2 * way)).start()
     kv_copy(v, kvm_r, mate).start()
 
-    wait_recv(queryz_recv.at[pl.ds(0, 3)], qz_r)
-    for d in (4, 3, 5, 2, 6, 1, 7):
-        remote(
-            queryz_recv.at[:, y_peer(d)], query_recv.at[y], q_s, q_r, seq=h * 8 + y_peer(d)
-        ).start()
-    query_recv[y] = queryz_recv[:, y]
 
     gains, rows = own_columns(gain), own_columns(hidden)
-    wait_recv(part_recv.at[pl.ds(0, 7)], part_r)
-    total = jnp.sum(part_recv[...].astype(F32), axis=0)
-    ends = total[128:160]
-    totals = [total[0:64], total[64:128], jnp.concatenate([ends, half_turn(ends)], axis=0)]
-    grads = [inv_rms * g * t - x * tilt for g, t, x in zip(gains, totals, rows)]
-    blocks[y, h] = packed(*grads).astype(BF16)
-
-    def z_copy(d, target, origin):
-        at = blocks.at[y, origin]
-        return remote(at, at, z_s, z_r.at[d], seq=target * 8 + y)
-
-    for d in (1, 3, 2):
-        z_copy(d, lax.rem(h + d, 4), h).start()
-
-    def ring_copy(way, k, e, block):
-        to = lax.rem(y + 1 + 6 * way, 8)
-        at = blocks.at[block, lax.rem(h + e, 4)]
-        return remote(at, at, ring_s, ring_r.at[way, k, e], seq=h * 8 + to)
-
-    def sent(way, k):
-        return lax.rem(y + (8 - k if way == 0 else k), 8)
-
-    def got(way, k):
-        return lax.rem(y + (7 - k if way == 0 else k + 1), 8)
-
-    def goes(way, k, e):
-        return k < 3 or (e < 2) == (way == 0)
-
-    for way in range(2):
-        ring_copy(way, 0, 0, y).start()
-
-    hidden_out[:, 0:128] = grads[0].astype(BF16)
-    hidden_out[:, 128:256] = grads[1].astype(BF16)
-    hidden_out[:, 256:320] = grads[2][:, 0:64].astype(BF16)
-    stores[1].start()
+
+    def grad(i, total):
+        return inv_rms * gains[i] * total - rows[i] * tilt
+
+    def z_copy(f, d, target, origin):
+        at = blocks.at[origin, portions[f]]
+        return remote(at, at, z_s, z_r.at[f, d], seq=target * 8 + y)
 
     def kv_next(kind):
         block = v if kind == 0 else beside
@@ -371,44 +367,60 @@
             kv_copy(far, kv_xx.at[way, kind], mate, slice(way, way + 1)).wait_recv()
         kv_copy(far, kvm_r, mate).start()
 
-    def ring_start(e):
-        z_copy(4 - e, h, lax.rem(h + e, 4)).wait_recv()
-        for way in range(2):
-            ring_copy(way, 0, e, y).start()
-
-    def ring_next(k, e):
-        for way in range(2):
-            if goes(way, k - 1, e):
-                ring_copy(way, k - 1, e, got(way, k - 1)).wait_recv()
-            if k < 4 and goes(way, k, e):
-                ring_copy(way, k, e, sent(way, k)).start()
-
+    def send_block(f):
+        for d in (2, 1, 3):
+            z_copy(f, d, lax.rem(h + d, 4), h).start()
+
+    wait_recv(part_recv.at[pl.ds(0, 7), portions[0]], part_r.at[0])
+    first_grad = grad(0, jnp.sum(part_recv[:, 0:64].astype(F32), axis=0))
+    blocks[h, 0:64, :] = first_grad.astype(BF16)
+    send_block(0)
+    hidden_out[:, 0:128] = first_grad.astype(BF16)
+    wait_recv(part_recv.at[pl.ds(0, 7), portions[1]], part_r.at[1])
+    total = jnp.sum(part_recv[:, 64:160].astype(F32), axis=0)
+    ends = total[64:96]
+    second_grad = grad(1, total[0:64])
+    third_grad = grad(2, jnp.concatenate([ends, half_turn(ends)], axis=0))
+    blocks[h, 64:160, :] = jnp.concatenate(
+        [second_grad, jnp.where(left, third_grad[0:32], half_turn(third_grad[32:64]))], axis=0
+    ).astype(BF16)
+    send_block(1)
+    hidden_out[:, 128:256] = second_grad.astype(BF16)
+    hidden_out[:, 256:320] = third_grad[:, 0:64].astype(BF16)
+    stores[1].start()
+
+    proj_next(2, 0)
     kv_copy(beside, kv_z, mate).wait_recv()
     for way in range(2):
         kv_copy(beside, kv_x.at[way, 1], around(v, 1 + 2 * way)).start()
     kv_copy(beside, kvm_r, mate).start()
     kv_next(0)
-    ring_next(1, 0)
-    ring_start(1)
-    ring_start(3)
+    proj_next(2, 1)
+    for f in range(2):
+        for d in (1, 3, 2):
+            z_copy(f, d, h, lax.rem(h + 4 - d, 4)).wait_recv()
+    x = blocks[...]
+    ends = x[:, 128:160]
+    keep = lax.broadcasted_iota(jnp.int32, ends.shape, 2) < 64
+    zero = jnp.zeros_like(ends)
+    ends = jnp.concatenate([jnp.where(keep, ends, zero), jnp.where(keep, zero, ends)], axis=1)
+    acts[:, 0:128] = x[:, 0:64].reshape(256, 128)
+    acts[:, 128:256] = x[:, 64:128].reshape(256, 128)
+    acts[:, 256:384] = ends.reshape(256, 128)
     kv_next(1)
-    ring_next(2, 0)
-    ring_start(2)
-    kv_last(0)
+    wait_recv(queryy_recv.at[pl.ds(0, 7)], qy_r)
+    for d in (2, 1, 3):
+        remote(
+            queryy_recv.at[:, z_peer(d)], query_recv.at[h], q_s, q_r, seq=z_peer(d) * 8 + y
+        ).start()
+    query_recv[h] = queryy_recv[:, h]
 
     def og_copy(j, b):
         return remote(og_give.at[b], og_mate.at[b], ogm_s, ogm_r.at[j], vocab=mate)
 
     def og_block(j, b):
-        x = blocks[b]
-        out = jnp.dot(x[:, 0:64].reshape(256, 128), proj[0:128, :], preferred_element_type=F32)
-        out += jnp.dot(x[:, 64:128].reshape(256, 128), proj[128:256, :], preferred_element_type=F32)
-        ends = x[:, 128:160].reshape(128, 128)
-        ends = [
-            jnp.dot(ends, proj_ends[i], preferred_element_type=F32).reshape(4, 32, STACK)
-            for i in range(2)
-        ]
-        out = out.reshape(4, 64, STACK) + jnp.concatenate(ends, axis=1)
+        projs[b, 320:384, :] = projs[b, 256:320, :]
+        out = jnp.dot(acts[...], projs[b], preferred_element_type=F32).reshape(4, 64, STACK)
         out = [out[i].reshape(8, 8, STACK) for i in range(4)]
         even = jnp.concatenate([first_halves(out[0], out[1]), first_halves(out[2], out[3])], axis=1)
         odd = jnp.concatenate([second_halves(out[0], out[1]), second_halves(out[2], out[3])], axis=1)
@@ -424,19 +436,30 @@
         def _(d):
             m = lax.rem(chip + d, 8)
             remote(
-                og_sum.at[b, m], og_recv.at[chip, b], og_s, og_r, vocab=2 * m + core
+                og_sum.at[b, m], og_recv.at[chip, b], og_s, og_r.at[j], vocab=2 * m + core
             ).start()
 
         og_recv[chip, b] = og_sum[b, chip]
 
+    def og_done(j, b):
+        wait_recv(og_recv.at[pl.ds(0, 7), b], og_r.at[j])
+        total = jnp.sum(og_recv[:, b].astype(F32), axis=0).astype(BF16)
+        if j == 0:
+            ogy_recv[y] = total
+        else:
+            ogy_send[b] = total
+            remote(ogy_send.at[b], ogy_recv.at[y], ogy_s, ogy_r, seq=h * 8 + b).start()
+
     order = [lax.rem(y + d, 8) for d in (0, 7, 1, 6, 2, 5, 3, 4)]
 
-    wait_recv(query_recv.at[pl.ds(0, 7)], q_r)
-    pairs = query_recv[...].astype(F32).reshape(16, 2, 16, 128)
-    even, odd = pairs[:, 0], pairs[:, 1]
-    query_rows[0:128, :] = first_halves(even[:, 0:8], odd[:, 0:8]).reshape(128, 128).astype(BF16)
-    query_rows[128:256, :] = second_halves(even[:, 0:8], odd[:, 0:8]).reshape(128, 128).astype(BF16)
-    query_rows[256:384, :] = first_halves(even[:, 8:16], odd[:, 8:16]).reshape(128, 128).astype(BF16)
+    def query_step():
+        wait_recv(query_recv.at[pl.ds(0, 3)], q_r)
+        x = query_recv[...].astype(F32)
+        for j in range(GROUP_HEADS):
+            part = x[:, :, 8 * (j // 2) : 8 * (j // 2) + 8]
+            join = first_halves if j % 2 == 0 else second_halves
+            part = jnp.concatenate([join(part[0], part[1]), join(part[2], part[3])], axis=1)
+            query_rows[ROWS * j : ROWS * j + ROWS, :] = part.reshape(ROWS, HEAD).astype(BF16)
 
     start = offset[0]
     r = lax.rem(lax.broadcasted_iota(jnp.int32, (1, STACK), 1), ROWS)
@@ -482,45 +505,51 @@
         for n in range(first, last):
             piece(n)
 
+    def pieces(first, last):
+        for n in range(first, last):
+            piece(n)
+
     og_block(0, order[0])
-    ring_next(1, 1)
-    ring_next(1, 3)
-    kv_last(1)
-    ring_next(3, 0)
-    ring_next(1, 2)
     og_block(1, order[1])
     og_block(2, order[2])
-    ring_next(2, 1)
+    proj_next(3, 0)
     og_pass(0, order[0])
-    ring_next(2, 3)
-    wait_recv(kv.at[:, :, 1 - core], kvm_r)
-    pieces(0, 3)
-    ring_next(4, 0)
-    ring_next(2, 2)
+    og_pass(1, order[1])
+    og_pass(2, order[2])
+    kv_last(0)
+    proj_next(3, 1)
     og_block(3, order[3])
-    og_pass(1, order[1])
-    ring_next(3, 1)
     og_block(4, order[4])
-    og_pass(2, order[2])
-    ring_next(3, 3)
-    pieces(3, 7)
-    ring_next(3, 2)
+    kv_last(1)
     og_block(5, order[5])
     og_pass(3, order[3])
     og_block(6, order[6])
     og_pass(4, order[4])
-    ring_next(4, 1)
-    ring_next(4, 3)
-    pieces(7, 10)
+    wait_recv(kv.at[:, :, 1 - core], kvm_r)
+    query_step()
+    pieces(0, 4)
     og_pass(5, order[5])
-    ring_next(4, 2)
+    proj_next(4, 0)
+    proj_next(4, 1)
     og_block(7, order[7])
     og_pass(6, order[6])
-    pieces(10, 18)
+    pieces(4, 8)
+    og_done(0, order[0])
+    og_done(1, order[1])
     og_pass(7, order[7])
+    og_done(2, order[2])
+    pieces(8, 11)
+    og_done(3, order[3])
+    pieces(11, 14)
+    og_done(4, order[4])
+    pieces(14, 16)
+    og_done(5, order[5])
+    pieces(16, 18)
+    og_done(6, order[6])
+    og_done(7, order[7])
     pieces(18, 24)
-    wait_recv(og_recv.at[pl.ds(0, 7)], og_r)
-    out = jnp.sum(og_recv[...].astype(F32), axis=0).reshape(ROWS, STACK).astype(BF16)
+    wait_recv(ogy_recv.at[pl.ds(0, 7)], ogy_r)
+    out = ogy_recv[...].reshape(ROWS, STACK)
     out_grad = jnp.concatenate([out[:, 0:128], out[:, 128:256], out[:, 256:384]], axis=0)
 
     def group(j):
@@ -625,13 +654,14 @@
     wait_send(part_recv.at[pl.ds(0, 7)], part_s)
     wait_send(og_mate, ogm_s)
     wait_send(og_recv.at[pl.ds(0, 7)], og_s)
+    wait_send(ogy_recv.at[pl.ds(0, 7)], ogy_s)
     wait_send(kvz_recv.at[pl.ds(0, 3)], kvz_s)
     wait_send(kvy_recv.at[pl.ds(0, 7)], kvy_s)
-    wait_send(queryz_recv.at[pl.ds(0, 3)], qz_s)
-    wait_send(query_recv.at[pl.ds(0, 7)], q_s)
+    wait_send(queryy_recv.at[pl.ds(0, 7)], qy_s)
+    wait_send(query_recv.at[pl.ds(0, 3)], q_s)
     wait_send(score_grad.at[pl.ds(0, 1280)], kv_s)
-    wait_send(blocks.at[0, pl.ds(0, 3)], z_s)
-    wait_send(blocks.at[pl.ds(0, 7)], ring_s)
+    wait_send(blocks.at[pl.ds(0, 3)], z_s)
+    wait_send(projs.at[pl.ds(0, 7), 0:320], proj_s)
     wait_send(dkv_mate, dkvm_s)
     wait_send(dkv_recv.at[:, pl.ds(0, 7)], dkv_s)
     wait_send(dqy_recv.at[pl.ds(0, 7)], dqy_s)
@@ -679,10 +709,11 @@
         v((1, TOK), F32), v((TOK, 320), BF16), v((4, 12288), BF16), v((2, 4, 1024), BF16),
         v((256, 2 * TOK), BF16), v((2 * TOK, D), F32), v((8, 128), F32), v((VOC, 8, 128), F32),
         v((2, 8, 160, 128), BF16), v((8, 160, 128), BF16), v((8, 160, 128), BF16), v((8, 160, 128), BF16),
-        v((8, 4, 160, 128), BF16), v((320, STACK), BF16), v((2, 128, STACK), BF16),
+        v((4, 160, 128), BF16), v((256, 384), BF16), v((8, 384, STACK), BF16),
         v((8, 8, 16, STACK), F32), v((8, 8, 16, STACK), BF16), v((8, 8, 16, STACK), BF16),
         v((8, 8, 16, STACK), BF16), v((8, 8, 16, STACK), BF16),
-        v((SEQ, 16, 128), F32), v((4, 8, 16, 128), BF16), v((4, 8, 16, 128), BF16), v((8, 4, 16, 128), BF16),
+        v((8, 16, STACK), BF16), v((8, 16, STACK), BF16),
+        v((SEQ, 16, 128), F32), v((8, 4, 16, 128), BF16), v((8, 4, 16, 128), BF16), v((4, 8, 16, 128), BF16),
         v((STACK, 128), BF16),
         v((4, 16, 128), F32), v((4, 16, 128), BF16), v((4, 16, 128), BF16),
         v((2, 32, 128), BF16), v((8, 32, 128), BF16), v((2, 8, 2, ROWS, 128), BF16),
@@ -693,8 +724,8 @@
         v((8, 32, 128), BF16), v((8, 32, 128), BF16), v((4, 16, 128), BF16), v((4, 16, 128), BF16),
     ]
     sizes = [
-        (8,), (4,), None, None, (2,), (2,), None, None, None, (4,), None, (2, 4, 4),
-        None, (8,), None, None, None, None, None, None, None, None, None, None,
+        (8,), (4,), None, None, (2,), (2,), None, (2,), None, (2, 4), None, (2, 4, 2),
+        None, (8,), None, (8,), None, None, None, None, None, None, None, None, None, None,
         None, None, (2, 2), (2, 2), None,
         None, None, None, None, None, (2, 4), None, (2,), None, None, None, None,
     ]
@@ -703,12 +734,15 @@
 
 def store(*refs):
     sems = refs[12]
-    for first, second in ((0, 8), (8, 4)):
-        copies = [pltpu.make_async_copy(refs[first + i], refs[second + i], sems.at[i]) for i in range(4)]
-        for copy in copies:
-            copy.start()
-        for copy in copies:
-            copy.wait()
+    ins = [pltpu.make_async_copy(refs[i], refs[8 + i], sems.at[i]) for i in range(4)]
+    outs = [pltpu.make_async_copy(refs[8 + i], refs[4 + i], sems.at[4 + i]) for i in range(4)]
+    for copy in ins:
+        copy.start()
+    for first, second in zip(ins, outs):
+        first.wait()
+        second.start()
+    for copy in outs:
+        copy.wait()
 
 
 def shards(hidden, norm_gain, head_weight, targets, out_proj, query, saved_key_value, offset):
@@ -737,7 +771,7 @@
         out_shape=outs,
         in_specs=[hbm] * 4,
         out_specs=(hbm,) * 4,
-        scratch_shapes=[pltpu.VMEM(x.shape, x.dtype) for x in outs] + [pltpu.SemaphoreType.DMA((4,))],
+        scratch_shapes=[pltpu.VMEM(x.shape, x.dtype) for x in outs] + [pltpu.SemaphoreType.DMA((8,))],
         compiler_params=pltpu.CompilerParams(vmem_limit_bytes=VMEM_BYTES),
     )(*results)
     return loss.reshape(TOK), hidden_grad, query_grad, kv_grad

time: 77.3 us -> 74.9 us (0.969)
  Pallas kernels: 75.9 us -> 73.2 us
    pallas_call x1, Pallas kernels: 74.2 us -> 71.5 us  [shards(): pl.pallas_call(body, out_shape=outs, in_specs=[hbm] * 7 + [pl.BlockSpec(m...]
where the time goes in v4:
time: 74.9 us; the launch traced here: 74.5 us
  Pallas kernels  73.2 us (98%)
  between operations  1.29 us (2%)
    pallas_call x1, Pallas kernels, shards(): pl.pallas_call(body, out_shape=outs, in_specs=[hbm] * 7 + [pl.BlockSpec(m...  71.5 us
    pallas_call x1, Pallas kernels, shards(): pl.pallas_call(store, out_shape=outs, in_specs=[hbm] * 4, out_specs=(hbm,...  1.64 us

profile of v4, /device:TPU:1, one launch (start us, length us, event | category | flops | bytes accessed | tf_op | source)
XLA Modules:
  0.0 74.5 jit_solution(8729134487975589300)
XLA Ops:
  1.3 71.5 %shard_map.111 = (f32[1,64]{1,0:T(1,128)}, bf16[64,320]{1,0:T(8,128)(2,1)}, bf16[4,12288]{1,0:T(4,128)(2,1)}, bf16[2,4,1024]{2,1,0:T(4,128)(2,1)}) custom-call(bf16[64,5120]{1,0:T(8,128)(2,1)} %hidden_in.1, f32[1,5120]{1,0:T(1,128)} %bitcast.5, bf16[256,5120]{1,0:T(8,128)(2,1)} %weight_in.1, s32[1,64]{1,0:T(1,128)} %bitcast.6, bf16[320,384]{1,0:T(8,128)(2,1)} %bitcast.4, ...), custom_call_target="tpu_custom_call" | custom-call | tf_op jit(solution)/shard_map/pallas_call | solution.py:756
  72.8 1.6 %shard_map.112 = (f32[1,64]{1,0:T(1,128)}, bf16[64,320]{1,0:T(8,128)(2,1)}, bf16[4,12288]{1,0:T(4,128)(2,1)}, bf16[2,4,1024]{2,1,0:T(4,128)(2,1)}) custom-call(f32[1,64]{1,0:T(1,128)} %get-tuple-element.12.refs_0_, bf16[64,320]{1,0:T(8,128)(2,1)} %get-tuple-element.13.refs_1_, bf16[4,12288]{1,0:T(4,128)(2,1)} %get-tuple-element.14.refs_2_, ...), custom_call_target="tpu_custom_call" | custom-call | tf_op jit(solution)/shard_map/pallas_call | solution.py:769

commit v5 on v4

--- a/solution.py
+++ b/solution.py
@@ -60,9 +60,9 @@
 
 
 def body(
-    hidden_in, gain_in, weight_in, targets_in, proj_in, query_in, key_value_in, offset,
-    loss_res, hidden_res, query_res, kv_res,
-    hidden, gain, weight, targets, query, key_value, loss_out, hidden_out, query_out, kv_out,
+    hidden_in, gain_in, weight_in, targets_in, proj_in, query, key_value, offset,
+    loss_res, hidden_res, query_out, kv_out,
+    hidden, gain, weight, targets, loss_out, hidden_out,
     grad_rows, part_raw, stat_send, stat_recv, part_send, part_mate, part_sum, part_recv,
     blocks, acts, projs, og_own, og_give, og_mate, og_sum, og_recv, ogy_send, ogy_recv,
     query_wide, query_send, queryy_recv, query_recv, query_rows, kv_wide, kvz_send, kvz_recv, kvy_send, kvy_recv, kv,
@@ -95,7 +95,7 @@
                 (hidden_in, hidden), (gain_in, gain), (targets_in, targets),
                 (weight_in.at[:, 0:2560], weight.at[:, 0:2560]),
                 (weight_in.at[:, 2560:5120], weight.at[:, 2560:5120]),
-                (query_in, query), (key_value_in, key_value), (proj_in, projs.at[y, 0:320]),
+                (proj_in, projs.at[y, 0:320]),
             ]
         )
     ]
@@ -127,7 +127,7 @@
     stores = [
         pltpu.make_async_copy(src, dst, out_s.at[i])
         for i, (src, dst) in enumerate(
-            [(loss_out, loss_res), (hidden_out, hidden_res), (query_out, query_res), (kv_out, kv_res)]
+            [(loss_out, loss_res), (hidden_out, hidden_res)]
         )
     ]
 
@@ -673,7 +673,6 @@
             for j in range(GROUP_HEADS):
                 lane = (GROUP_HEADS * t + j) * HEAD
                 query_out[:, lane : lane + HEAD] = x[4 * j : 4 * j + 4].astype(BF16)
-        stores[2].start()
 
     wait_recv(foldy_recv.at[pl.ds(0, 7)], foldy_r)
     sums = []
@@ -695,7 +694,6 @@
         x = foldz_recv[k // 2].astype(F32)[8 * (k % 2) : 8 * (k % 2) + 8]
         kv_out[0, :, k * HEAD : k * HEAD + HEAD] = x[0:4].astype(BF16)
         kv_out[1, :, k * HEAD : k * HEAD + HEAD] = x[4:8].astype(BF16)
-    stores[3].start()
     for copy in stores:
         copy.wait()
 
@@ -705,8 +703,7 @@
     dma = pltpu.SemaphoreType.DMA
     buffers = [
         v((TOK, D), BF16), v((1, D), F32), v((256, D), BF16), v((1, TOK), jnp.int32),
-        v((4, 12288), BF16), v((2, 4, 1024), BF16),
-        v((1, TOK), F32), v((TOK, 320), BF16), v((4, 12288), BF16), v((2, 4, 1024), BF16),
+        v((1, TOK), F32), v((TOK, 320), BF16),
         v((256, 2 * TOK), BF16), v((2 * TOK, D), F32), v((8, 128), F32), v((VOC, 8, 128), F32),
         v((2, 8, 160, 128), BF16), v((8, 160, 128), BF16), v((8, 160, 128), BF16), v((8, 160, 128), BF16),
         v((4, 160, 128), BF16), v((256, 384), BF16), v((8, 384, STACK), BF16),
@@ -724,7 +721,7 @@
         v((8, 32, 128), BF16), v((8, 32, 128), BF16), v((4, 16, 128), BF16), v((4, 16, 128), BF16),
     ]
     sizes = [
-        (8,), (4,), None, None, (2,), (2,), None, (2,), None, (2, 4), None, (2, 4, 2),
+        (6,), (2,), None, None, (2,), (2,), None, (2,), None, (2, 4), None, (2, 4, 2),
         None, (8,), None, (8,), None, None, None, None, None, None, None, None, None, None,
         None, None, (2, 2), (2, 2), None,
         None, None, None, None, None, (2, 4), None, (2,), None, None, None, None,
@@ -733,19 +730,12 @@
 
 
 def store(*refs):
-    sems = refs[12]
-    ins = [pltpu.make_async_copy(refs[i], refs[8 + i], sems.at[i]) for i in range(4)]
-    outs = [pltpu.make_async_copy(refs[8 + i], refs[4 + i], sems.at[4 + i]) for i in range(4)]
-    for copy in ins:
-        copy.start()
-    for first, second in zip(ins, outs):
-        first.wait()
-        second.start()
-    for copy in outs:
-        copy.wait()
+    for src, dst in zip(refs[:4], refs[4:]):
+        dst[...] = src[...]
 
 
 def shards(hidden, norm_gain, head_weight, targets, out_proj, query, saved_key_value, offset):
+    vmem = pl.BlockSpec(memory_space=pltpu.VMEM)
     hbm = pl.BlockSpec(memory_space=pltpu.HBM)
     outs = (
         jax.ShapeDtypeStruct((1, TOK), F32),
@@ -756,8 +746,8 @@
     results = pl.pallas_call(
         body,
         out_shape=outs,
-        in_specs=[hbm] * 7 + [pl.BlockSpec(memory_space=pltpu.SMEM)],
-        out_specs=(hbm,) * 4,
+        in_specs=[hbm] * 5 + [vmem] * 2 + [pl.BlockSpec(memory_space=pltpu.SMEM)],
+        out_specs=(hbm, hbm, vmem, vmem),
         scratch_shapes=scratch(),
         compiler_params=pltpu.CompilerParams(
             collective_id=0, has_side_effects=True, vmem_limit_bytes=VMEM_BYTES
@@ -769,9 +759,8 @@
     loss, hidden_grad, query_grad, kv_grad = pl.pallas_call(
         store,
         out_shape=outs,
-        in_specs=[hbm] * 4,
-        out_specs=(hbm,) * 4,
-        scratch_shapes=[pltpu.VMEM(x.shape, x.dtype) for x in outs] + [pltpu.SemaphoreType.DMA((8,))],
+        in_specs=[vmem] * 4,
+        out_specs=(vmem,) * 4,
         compiler_params=pltpu.CompilerParams(vmem_limit_bytes=VMEM_BYTES),
     )(*results)
     return loss.reshape(TOK), hidden_grad, query_grad, kv_grad

time: 74.9 us -> 76 us (1.015)
  Pallas kernels: 73.2 us -> 74.5 us
    pallas_call x2, Pallas kernels: 73.2 us -> 74.5 us  [the longest x1 72.9 us: shards(): pl.pallas_call(body, out_shape=outs, in_specs=[hbm] * 5 + [vmem] * 2 + [p...]
where the time goes in v5:
time: 76 us; the launch traced here: 75.8 us
  Pallas kernels  74.5 us (98%)
  between operations  1.29 us (2%)
    pallas_call x1, Pallas kernels, shards(): pl.pallas_call(body, out_shape=outs, in_specs=[hbm] * 5 + [vmem] * 2 + [p...  72.9 us
    pallas_call x1, Pallas kernels, shards(): pl.pallas_call(store, out_shape=outs, in_specs=[vmem] * 4, out_specs=(vme...  1.6 us

profile of v5, /device:TPU:1, one launch (start us, length us, event | category | flops | bytes accessed | tf_op | source)
XLA Modules:
  0.0 75.8 jit_solution(2625975930469625165)
XLA Ops:
  1.3 72.9 %shard_map.111 = (f32[1,64]{1,0:T(1,128)}, bf16[64,320]{1,0:T(8,128)(2,1)}, bf16[4,12288]{1,0:T(4,128)(2,1)}, bf16[2,4,1024]{2,1,0:T(4,128)(2,1)}) custom-call(bf16[64,5120]{1,0:T(8,128)(2,1)} %hidden_in.1, f32[1,5120]{1,0:T(1,128)} %bitcast.5, bf16[256,5120]{1,0:T(8,128)(2,1)} %weight_in.1, s32[1,64]{1,0:T(1,128)} %bitcast.6, bf16[320,384]{1,0:T(8,128)(2,1)} %bitcast.4, ...), custom_call_target="tpu_custom_call" | custom-call | tf_op jit(solution)/shard_map/pallas_call | solution.py:746
  74.2 1.6 %shard_map.112 = (f32[1,64]{1,0:T(1,128)}, bf16[64,320]{1,0:T(8,128)(2,1)}, bf16[4,12288]{1,0:T(4,128)(2,1)}, bf16[2,4,1024]{2,1,0:T(4,128)(2,1)}) custom-call(f32[1,64]{1,0:T(1,128)} %get-tuple-element.12.refs_0_, bf16[64,320]{1,0:T(8,128)(2,1)} %get-tuple-element.13.refs_1_, bf16[4,12288]{1,0:T(4,128)(2,1)} %get-tuple-element.14.refs_2_, ...), custom_call_target="tpu_custom_call" | custom-call | tf_op jit(solution)/shard_map/pallas_call | solution.py:759

commit v6 on v4

--- a/solution.py
+++ b/solution.py
@@ -432,8 +432,7 @@
         og_copy(j, b).wait_recv()
         og_sum[b] = (og_own[b] + og_mate[b].astype(F32)).astype(BF16)
 
-        @pl.loop(1, 8)
-        def _(d):
+        for d in (4, 5, 3, 2, 6, 7, 1):
             m = lax.rem(chip + d, 8)
             remote(
                 og_sum.at[b, m], og_recv.at[chip, b], og_s, og_r.at[j], vocab=2 * m + core
@@ -553,7 +552,7 @@
     out_grad = jnp.concatenate([out[:, 0:128], out[:, 128:256], out[:, 256:384]], axis=0)
 
     def group(j):
-        return lax.rem(chip // 2 + 1 + j, 4)
+        return lax.rem(chip // 2 + (2, 1, 3, 0)[j], 4)
 
     def group_keys(j):
         return pl.ds(pl.multiple_of(group(j) * 512, 512), 512)

time: 74.9 us -> 74.6 us (level)
  no operation moved by 1% of the time
where the time goes in v6:
time: 74.6 us; the launch traced here: 74.4 us
  Pallas kernels  73.1 us (98%)
  between operations  1.29 us (2%)
    pallas_call x1, Pallas kernels, shards(): pl.pallas_call(body, out_shape=outs, in_specs=[hbm] * 7 + [pl.BlockSpec(m...  71.5 us
    pallas_call x1, Pallas kernels, shards(): pl.pallas_call(store, out_shape=outs, in_specs=[hbm] * 4, out_specs=(hbm,...  1.64 us

profile of v6, /device:TPU:1, one launch (start us, length us, event | category | flops | bytes accessed | tf_op | source)
XLA Modules:
  0.0 74.4 jit_solution(10566838508321592230)
XLA Ops:
  1.3 71.5 %shard_map.111 = (f32[1,64]{1,0:T(1,128)}, bf16[64,320]{1,0:T(8,128)(2,1)}, bf16[4,12288]{1,0:T(4,128)(2,1)}, bf16[2,4,1024]{2,1,0:T(4,128)(2,1)}) custom-call(bf16[64,5120]{1,0:T(8,128)(2,1)} %hidden_in.1, f32[1,5120]{1,0:T(1,128)} %bitcast.5, bf16[256,5120]{1,0:T(8,128)(2,1)} %weight_in.1, s32[1,64]{1,0:T(1,128)} %bitcast.6, bf16[320,384]{1,0:T(8,128)(2,1)} %bitcast.4, ...), custom_call_target="tpu_custom_call" | custom-call | tf_op jit(solution)/shard_map/pallas_call | solution.py:755
  72.8 1.6 %shard_map.112 = (f32[1,64]{1,0:T(1,128)}, bf16[64,320]{1,0:T(8,128)(2,1)}, bf16[4,12288]{1,0:T(4,128)(2,1)}, bf16[2,4,1024]{2,1,0:T(4,128)(2,1)}) custom-call(f32[1,64]{1,0:T(1,128)} %get-tuple-element.12.refs_0_, bf16[64,320]{1,0:T(8,128)(2,1)} %get-tuple-element.13.refs_1_, bf16[4,12288]{1,0:T(4,128)(2,1)} %get-tuple-element.14.refs_2_, ...), custom_call_target="tpu_custom_call" | custom-call | tf_op jit(solution)/shard_map/pallas_call | solution.py:768
